TPU v7x, 32 devices: a whole 2x2x4 slice. The times are simulated.
32 devices in a mesh: section: 16 (over z, y, x), expert: 2 (over core).
Axes of the slice: x: 2, y: 2, z: 4, core: 2. Of those that a mesh axis runs over, the one named last changes fastest.
Arguments:
- state: bfloat16 [16, 2048, 3584], P('section', 'expert'), may hold values from -6 to 6
- norm_gain: float32 [16, 3584], P('section'), may hold values from 0.1 to 1.9
- router: bfloat16 [16, 3584, 128], P('section'), may hold values from -0.1875 to 0.1875
- w_gate: bfloat16 [16, 3584, 1024], P('section', None, 'expert'), may hold values from -0.09375 to 0.09375
- w_up: bfloat16 [16, 3584, 1024], P('section', None, 'expert'), may hold values from -0.09375 to 0.09375
- w_down: bfloat16 [16, 1024, 3584], P('section', 'expert'), may hold values from -0.25 to 0.25
- route_ids: int32 [1, 16, 2048, 8], P(None, 'section', 'expert'), may hold values from 0 to 127, as said below
Outputs:
- state_out: bfloat16 [16, 2048, 3584], P('section', 'expert')
Inputs may be any that keep to these rules, and one draw needn't show every extreme that they name: `route_ids`: each row names 8 different experts; expert 0 is the expert whose weights are given.
All inputs are finite; a program needn't handle non-finite values.
Results may differ from a plain program's by a relative error of at most 0.002.
Values may be sent and summed in bfloat16 or wider, within the bound.
A program may use at most 128 MiB of HBM per device.

v0:
```python
import jax
import jax.numpy as jnp
from jax import lax
from jax.sharding import PartitionSpec as P


def passed_along(x, axis, by):
    devices = lax.axis_size(axis)
    return lax.ppermute(x, axis, [(i, (i + by) % devices) for i in range(devices)])


def expert_part(piece, gate_dev, up_dev, down_dev):
    gate = jnp.dot(piece, gate_dev, preferred_element_type=jnp.float32)
    upper = jnp.dot(piece, up_dev, preferred_element_type=jnp.float32)
    active = (jax.nn.silu(gate) * upper).astype(jnp.bfloat16)
    partial_out = jnp.dot(active, down_dev, preferred_element_type=jnp.float32)
    return lax.optimization_barrier(partial_out.astype(jnp.bfloat16)).astype(jnp.float32)


def place_rows(slot_rows, row_slot):
    valid = row_slot >= 0
    safe_slot = jnp.where(valid, row_slot, 0)
    taken = jnp.take(slot_rows, safe_slot, axis=0)
    return jnp.where(valid[:, None], taken, 0.0)


def local(state, norm_gain, router, w_gate, w_up, w_down, route_ids):
    gate_dev = w_gate[0]
    up_dev = w_up[0]
    down_dev = w_down[0]
    gain = norm_gain[0]
    table = router[0]
    current = state[0]
    rows = current.shape[0]
    capacity = rows // 8
    slot_iota = jnp.arange(capacity)[:, None]
    expert_iota = jnp.arange(table.shape[1])
    h32 = current.astype(jnp.float32)
    var = jnp.mean(h32 * h32, axis=-1, keepdims=True)
    normed = (h32 * lax.rsqrt(var + 1e-06) * gain).astype(jnp.bfloat16)
    scores = jax.nn.sigmoid(jnp.dot(normed, table, preferred_element_type=jnp.float32))
    ids = route_ids[0, 0]
    picked = jnp.sum((ids[:, :, None] == expert_iota[None, None, :]).astype(jnp.float32), axis=1)
    weight = 2.5 * scores[:, 0] * picked[:, 0] / jnp.sum(scores * picked, axis=-1)
    chosen = jnp.sum((ids == 0).astype(jnp.int32), axis=-1)
    slot = jnp.cumsum(chosen) - chosen
    kept = (chosen > 0) & (slot < capacity)
    row_slot = jnp.where(kept, slot, -1)
    onehot = (kept[None, :] & (slot[None, :] == slot_iota)).astype(jnp.bfloat16)
    packed = jnp.dot(onehot, normed, preferred_element_type=jnp.float32).astype(jnp.bfloat16)
    partials = expert_part(
        lax.all_gather(packed, "expert", axis=0, tiled=True), gate_dev, up_dev, down_dev
    )
    summed = lax.psum_scatter(
        partials.astype(jnp.bfloat16), "expert", scatter_dimension=0, tiled=True
    ).astype(jnp.float32)
    share = jnp.dot(onehot.astype(jnp.float32), weight, precision=lax.Precision.HIGHEST)
    scaled = summed * share[:, None]
    delta = place_rows(scaled, row_slot)
    current = passed_along((h32 + delta).astype(jnp.bfloat16), "section", 1)
    return current[None]


def solution(mesh):
    return jax.shard_map(
        local,
        mesh=mesh,
        in_specs=(
            P("section", "expert", None),
            P("section", None),
            P("section", None, None),
            P("section", None, "expert"),
            P("section", None, "expert"),
            P("section", "expert", None),
            P(None, "section", "expert", None),
        ),
        out_specs=P("section", "expert", None),
        check_vma=False,
    )
```

profile of v0, /device:TPU:0, one launch (start us, length us, event | category | flops | bytes accessed | tf_op | source)
XLA Modules:
  0.0 248.9 jit_solution(5898402053204904240)
XLA Ops:
  6.5 0.0 copy-start
  6.5 0.0 copy-start.2
  6.5 0.0 all-gather.2.cloned.1.call-start
  6.5 0.9 convert_reduce_fusion.1
  7.4 0.3 reduce-window.9
  7.7 0.1 slice.13
  7.8 0.1 slice_reduce_fusion
  7.9 4.6 %fusion.3 = f32[1024]{0:T(1024)S(1)} fusion(bf16[1,1024,3584]{2,1,0:T(8,128)(2,1)} %param.7), kind=kLoop, calls=%fused_computation.6 | loop fusion | flops 11009024 | bytes 7344128 | tf_op jit(solution)/shard_map/reduce_sum | solution.py:39
  12.5 0.1 select_compare_fusion
  12.6 0.0 copy-done.2
  12.6 6.5 %fusion.18 = bf16[128,3584]{1,0:T(8,128)(2,1)} fusion(bf16[1,1024,3584]{2,1,0:T(8,128)(2,1)} %param.7, f32[3584]{0:T(1024)S(1)} %reduce.1, f32[1024]{0:T(1024)S(1)} %add_rsqrt_fusion, s32[1024]{0:T(1024)S(1)} %get-tuple-element.7, pred[1024]{0:T(1024)(128)(4,1)S(1)} %get-tuple-element.6), kind=kOutput, calls=%fused_computation.20 | convolution fusion | flops 954925056 | bytes 8281088 | tf_op jit(solution)/shard_map/dot_general | solution.py:50
  19.1 0.0 all-gather.2.cloned.1.call-update
  19.1 0.0 reduce-scatter.2.cloned.1.call-start
  19.2 13.0 %all-gather.2.cloned.1.call-done = bf16[256,3584]{1,0:T(8,128)(2,1)} async-done(((bf16[128,3584]{1,0:T(8,128)(2,1)}), bf16[256,3584]{1,0:T(8,128)(2,1)}) %all-gather.2.cloned.1.call-update) | async-done | bytes 1835024 | tf_op jit(solution)/shard_map/all_gather | solution.py:52
  32.2 3.7 %fusion.24 = f32[256,512]{1,0:T(8,128)S(1)} fusion(bf16[256,3584]{1,0:T(8,128)(2,1)} %all-gather.2.cloned.1.call-done, bf16[1,3584,512]{2,1,0:T(8,128)(2,1)} %param.10), kind=kOutput, calls=%fused_computation.26 | convolution fusion | flops 939524096 | bytes 6029312 | tf_op jit(solution)/shard_map/dot_general | solution.py:13
  35.9 0.0 copy-start.1
  35.9 7.1 %convolution_convert_fusion = bf16[256,3584]{1,0:T(8,128)(2,1)} fusion(bf16[1,512,3584]{2,1,0:T(8,128)(2,1)} %param.12, bf16[256,3584]{1,0:T(8,128)(2,1)} %all-gather.2.cloned.1.call-done, bf16[1,3584,512]{2,1,0:T(8,128)(2,1)} %param.11, f32[256,512]{1,0:T(8,128)S(1)} %fusion.24), kind=kOutput, calls=%fused_computation.19 | convolution fusion | flops 1880752128 | bytes 11534336 | tf_op jit(solution)/shard_map/dot_general | solution.py:16
  43.0 0.0 reduce-scatter.2.cloned.1.call-update
  43.0 0.0 copy-done.1
  43.0 0.2 copy.10
  43.2 5.7 %convert_reduce_fusion = f32[1024,128]{1,0:T(8,128)S(1)} fusion(s32[1024,8]{1,0:T(8,128)S(1)} %copy.10), kind=kLoop, calls=%fused_computation.21 | loop fusion | flops 3014656 | bytes 557056 | tf_op jit(solution)/shard_map/reduce_sum | solution.py:43
  49.0 0.2 copy.11
  49.2 0.0 copy-done
  49.2 5.9 %multiply_reduce_fusion = (f32[1024]{0:T(1024)S(1)}, f32[1024,128]{0,1:T(8,128)S(1)}) fusion(f32[1024,128]{0,1:T(8,128)S(1)} %copy.11, bf16[1,3584,128]{2,1,0:T(8,128)(2,1)S(1)} %copy-done, bf16[1,1024,3584]{2,1,0:T(8,128)(2,1)} %param.7, f32[3584]{0:T(1024)S(1)} %reduce.1, f32[1024]{0:T(1024)S(1)} %add_rsqrt_fusion), kind=kOutput, calls=%fused_computation.37 | convolution fusion | flops 954858496 | bytes 9328640 | tf_op jit(solution)/shard_map/dot_general | solution.py:41
  55.2 0.3 convolution_bitcast_fusion
  55.6 0.0 reduce-scatter.2.cloned.1.call-done
  55.6 1.4 convert_multiply_fusion.1
  57.0 8.9 %gather_fusion = f32[1024,3584]{1,0:T(8,128)} fusion(f32[128,3584]{1,0:T(8,128)S(1)} %convert_multiply_fusion.1, s32[1024]{0:T(1024)S(1)} %broadcast_clamp_fusion), kind=kCustom, calls=%fused_computation | custom fusion | bytes 29364224 | tf_op jit(solution)/shard_map/jit(_take)/gather | solution.py:23
  65.9 9.2 %fusion.6 = bf16[1024,3584]{1,0:T(8,128)(2,1)S(1)} fusion(bf16[1,1024,3584]{2,1,0:T(8,128)(2,1)} %param.7, f32[1024,3584]{1,0:T(8,128)} %gather_fusion, pred[1024]{0:T(1024)(128)(4,1)S(1)} %compare_and_fusion, pred[1024]{0:T(1024)(128)(4,1)S(1)} %get-tuple-element.5), kind=kLoop, calls=%fused_computation.9 | loop fusion | flops 18350080 | bytes 29362176 | tf_op jit(solution)/shard_map/convert_element_type | solution.py:60
  75.1 1.8 collective-permute-start
  76.9 162.1 %collective-permute-done = bf16[1024,3584]{1,0:T(8,128)(2,1)S(1)} collective-permute-done((bf16[1024,3584]{1,0:T(8,128)(2,1)S(1)}, bf16[1024,3584]{1,0:T(8,128)(2,1)S(1)}, u32[]{:S(2)}, u32[]{:S(2)}) %collective-permute-start) | collective-permute-done | bytes 7340064 | tf_op jit(solution)/shard_map/ppermute | solution.py:9
  239.0 3.0 %copy.14 = bf16[1,1024,3584]{2,1,0:T(8,128)(2,1)} copy(bf16[1,1024,3584]{2,1,0:T(8,128)(2,1)S(1)} %bitcast.69) | data formatting | bytes 14680064
  (8 shorter events, 0.1 us)
Async XLA Ops:
  6.5 42.7 %copy-start = (bf16[1,3584,128]{2,1,0:T(8,128)(2,1)S(1)}, bf16[1,3584,128]{2,1,0:T(8,128)(2,1)}, u32[]{:S(2)}) copy-start(bf16[1,3584,128]{2,1,0:T(8,128)(2,1)} %param.9) | copy-start | bytes 2752516
  6.5 6.1 %copy-start.2 = (f32[1,3584]{1,0:T(1,128)S(1)}, f32[1,3584]{1,0:T(1,128)}, u32[]{:S(2)}) copy-start(f32[1,3584]{1,0:T(1,128)} %param.8) | copy-start | bytes 43012
  6.5 25.6 %all-gather.2.cloned.1.call-start = ((), (), s32[]{:S(2)}) async-start(), calls=%async_computation.1 | async-start | bytes 2752512 | tf_op jit(solution)/shard_map/all_gather | solution.py:52
  19.1 36.5 %reduce-scatter.2.cloned.1.call-start = ((), (), s32[]{:S(2)}) async-start(), calls=%async_computation.2 | async-start | bytes 2752512 | tf_op jit(solution)/shard_map/reduce_scatter | solution.py:54
  35.9 7.1 %copy-start.1 = (s32[1,1,1024,8]{2,3,1,0:T(8,128)S(1)}, s32[1,1,1024,8]{2,3,1,0:T(8,128)}, u32[]{:S(2)}) copy-start(s32[1,1,1024,8]{2,3,1,0:T(8,128)} %param.13) | copy-start | bytes 98308
  75.1 163.9 %collective-permute-start = (bf16[1024,3584]{1,0:T(8,128)(2,1)S(1)}, bf16[1024,3584]{1,0:T(8,128)(2,1)S(1)}, u32[]{:S(2)}, u32[]{:S(2)}) collective-permute-start(bf16[1024,3584]{1,0:T(8,128)(2,1)S(1)} %fusion.6), channel_id=1, source_target_pairs={{0,2},{2,4},{4,6},{6,8},{8,10},{10,12},{12,14},{14,16},{16,18},{18... | collective-permute-start | bytes 22020104 | tf_op jit(solution)/shard_map/ppermute | solution.py:9
Sparse Core Ops, SparseCore 0:
  19.2 12.8 all-gather.1
  43.1 10.5 reduce-scatter.1
where the time goes:
time: 249 us
  waiting for transfers between devices  175 us (70%)
  matrix products  23.5 us (9%)
  other arithmetic  22.3 us (9%)
  between operations  13.5 us (5%)
  local copies, waits for them, and re-layouts  12.5 us (5%)
    ppermute x1, waiting for transfers between devices, passed_along(): lax.ppermute(x, axis, [(i, (i + by) % devices) for i in range(devices)])  162 us
    all_gather x1, waiting for transfers between devices, local(): lax.all_gather(packed, 'expert', axis=0, tiled=True)  13 us
    convert_element_type x1, other arithmetic, local(): current = passed_along((h32 + delta).astype(jnp.bfloat16), 'section', 1)  9.21 us
    gather x1, local copies, waits for them, and re-layouts, place_rows(): taken = jnp.take(slot_rows, safe_slot, axis=0)  8.87 us
    dot_general x1, matrix products, expert_part(): partial_out = jnp.dot(active, down_dev, preferred_element_type=jnp.float32)  7.11 us
    dot_general x1, matrix products, local(): jnp.dot(onehot, normed, preferred_element_type=jnp.float32)  6.45 us
    dot_general x1, matrix products, local(): jnp.dot(normed, table, preferred_element_type=jnp.float32)  5.93 us
    reduce_sum x1, other arithmetic, local(): jnp.sum((ids[:, :, None] == expert_iota[None, None, :]).astype(jnp.float3...  5.75 us
  transfers between devices with their start and end apart: 3, of which 2 were waited for; matrix products, arithmetic and copies ran while one was open for 5% of the time, Pallas kernels for 0%

commit v1 on v0

v1 whole, which is shorter than its diff:
```python
import functools

import jax
import jax.numpy as jnp
from jax import lax
from jax.experimental import pallas as pl
from jax.experimental.pallas import tpu as pltpu
from jax.sharding import PartitionSpec as P

VMEM_LIMIT = 56 * 1024 * 1024
CHUNKS = (1, 1, 2, 3)
NOWHERE = -(1 << 20)


def passed_along(x, axis, by):
    devices = lax.axis_size(axis)
    return lax.ppermute(x, axis, [(i, (i + by) % devices) for i in range(devices)])


def after(x, done):
    return lax.optimization_barrier((x, done))[0]


def onehot_to(pos, base, size):
    places = lax.broadcasted_iota(jnp.int32, (size, pos.shape[1]), 0) + base
    return jnp.where(places == pos, 1.0, 0.0).astype(jnp.bfloat16)


def pack_kernel(first, pos_a, pos_b, rows_a, rows_b, out):
    size = out.shape[0]
    base = (pl.program_id(0) + first) * size
    total = jnp.dot(onehot_to(pos_a[...], base, size), rows_a[...], preferred_element_type=jnp.float32)
    total += jnp.dot(onehot_to(pos_b[...], base, size), rows_b[...], preferred_element_type=jnp.float32)
    out[...] = total.astype(out.dtype)


def pack(h, pos, first, tiles, size):
    width = h.shape[1]
    return pl.pallas_call(
        functools.partial(pack_kernel, first),
        grid=(tiles,),
        in_specs=[
            pl.BlockSpec((1, size), lambda i: (0, i + first)),
            pl.BlockSpec((1, size), lambda i: (0, i + first + 1)),
            pl.BlockSpec((size, width), lambda i: (i + first, 0)),
            pl.BlockSpec((size, width), lambda i: (i + first + 1, 0)),
        ],
        out_specs=pl.BlockSpec((size, width), lambda i: (i, 0)),
        out_shape=jax.ShapeDtypeStruct((tiles * size, width), h.dtype),
        compiler_params=pltpu.CompilerParams(vmem_limit_bytes=VMEM_LIMIT),
        cost_estimate=pl.CostEstimate(
            flops=4 * tiles * size * size * width, bytes_accessed=4 * tiles * size * width, transcendentals=0
        ),
        name="pack_rows",
    )(pos, pos, h, h)


def pack_last_kernel(base, pos, rows, out, total):
    step = pl.program_id(0)
    part = jnp.dot(onehot_to(pos[...], base, out.shape[0]), rows[...], preferred_element_type=jnp.float32)

    @pl.when(step == 0)
    def _():
        total[...] = part

    @pl.when(step > 0)
    def _():
        total[...] += part

    @pl.when(step == pl.num_programs(0) - 1)
    def _():
        out[...] = total[...].astype(out.dtype)


def pack_last(h, pos, base, size):
    rows, width = h.shape
    step = 2 * size
    return pl.pallas_call(
        functools.partial(pack_last_kernel, base),
        grid=(rows // step,),
        in_specs=[
            pl.BlockSpec((1, step), lambda i: (0, i)),
            pl.BlockSpec((step, width), lambda i: (i, 0)),
        ],
        out_specs=pl.BlockSpec((size, width), lambda i: (0, 0)),
        out_shape=jax.ShapeDtypeStruct((size, width), h.dtype),
        scratch_shapes=[pltpu.VMEM((size, width), jnp.float32)],
        compiler_params=pltpu.CompilerParams(vmem_limit_bytes=VMEM_LIMIT),
        cost_estimate=pl.CostEstimate(
            flops=2 * size * rows * width, bytes_accessed=2 * rows * width, transcendentals=0
        ),
        name="pack_last",
    )(pos, h)


def unpack_kernel(first, start, end, has_prev, *refs):
    if has_prev:
        pos, before, here_a, here_b, last, _, out = refs
    else:
        pos, here_a, here_b, last, out = refs
    size = out.shape[0]
    tile = pl.program_id(0) + first
    sources = [
        (here_a, jnp.where(tile - 1 >= start, tile - 1, NOWHERE)),
        (here_b, jnp.where(tile < end, tile, NOWHERE)),
        (last, 7),
    ]
    if has_prev:
        sources.append((before, jnp.where(tile - 1 < start, start - 1, NOWHERE)))
    total = None
    for ref, place in sources:
        onehot = onehot_to(pos[...], place * size, size)
        part = lax.dot_general(
            onehot, ref[...], (((0,), (0,)), ((), ())), preferred_element_type=jnp.float32
        )
        total = part if total is None else total + part
    out[...] = total.astype(out.dtype)


def unpack(pos, before, here, last, out, first, tiles, start, rows, size):
    width = here.shape[1]
    count = here.shape[0] // size
    end = start + count
    specs = [pl.BlockSpec((1, size), lambda i: (0, i + first))]
    args = [pos]
    if before is not None:
        specs.append(pl.BlockSpec((size, width), lambda i: (before.shape[0] // size - 1, 0)))
        args.append(before)
    specs += [
        pl.BlockSpec((size, width), lambda i: (jnp.clip(i + first - 1 - start, 0, count - 1), 0)),
        pl.BlockSpec((size, width), lambda i: (jnp.clip(i + first - start, 0, count - 1), 0)),
        pl.BlockSpec((size, width), lambda i: (0, 0)),
    ]
    args += [here, here, last]
    aliases = {}
    if out is not None:
        aliases = {len(args): 0}
        specs.append(pl.BlockSpec(memory_space=pl.ANY))
        args.append(out)
    return pl.pallas_call(
        functools.partial(unpack_kernel, first, start, end, before is not None),
        grid=(tiles,),
        in_specs=specs,
        out_specs=pl.BlockSpec((size, width), lambda i: (i + first, 0)),
        out_shape=jax.ShapeDtypeStruct((rows, width), here.dtype),
        input_output_aliases=aliases,
        compiler_params=pltpu.CompilerParams(vmem_limit_bytes=VMEM_LIMIT),
        cost_estimate=pl.CostEstimate(
            flops=6 * tiles * size * size * width, bytes_accessed=6 * tiles * size * width, transcendentals=0
        ),
        name="unpack_rows",
    )(*args)


def expert_part(piece, gate_dev, up_dev, down_dev):
    gate = jnp.dot(piece, gate_dev, preferred_element_type=jnp.float32)
    upper = jnp.dot(piece, up_dev, preferred_element_type=jnp.float32)
    active = (jax.nn.silu(gate) * upper).astype(jnp.bfloat16)
    partial_out = jnp.dot(active, down_dev, preferred_element_type=jnp.float32)
    return lax.optimization_barrier(partial_out.astype(jnp.bfloat16))


def local(state, norm_gain, router, w_gate, w_up, w_down, route_ids):
    h = state[0]
    rows = h.shape[0]
    size = rows // 8
    raw_rows = rows - size
    ids = route_ids[0, 0]

    chosen = jnp.sum((ids == 0).astype(jnp.int32), axis=-1)
    slot = jnp.cumsum(chosen) - chosen
    kept = (chosen > 0) & (slot < size)
    count = jnp.minimum(jnp.sum(chosen), size)
    other = jnp.arange(rows, dtype=jnp.int32) - jnp.minimum(slot, size)
    pos = jnp.where(kept, raw_rows + slot, jnp.where(other < raw_rows, other, other + count))
    pos = pos.astype(jnp.int32)[None, :]

    packed, arrived = [], []
    start = 0
    for tiles in CHUNKS:
        packed.append(pack(h, pos, start, tiles, size))
        start += tiles
    moved_pos = passed_along(pos, "section", 1)
    arrived.append(passed_along(packed[0], "section", 1))
    arrived.append(passed_along(packed[1], "section", 1))
    packed[2] = after(packed[2], arrived[0])
    arrived.append(passed_along(packed[2], "section", 1))
    last = pack_last(h, after(pos, packed[1]), raw_rows, size)

    last_ids = jnp.dot(
        onehot_to(pos, raw_rows, size), ids.astype(jnp.bfloat16), preferred_element_type=jnp.float32
    )
    last32 = last.astype(jnp.float32)
    var = jnp.mean(last32 * last32, axis=-1, keepdims=True)
    normed = (last32 * lax.rsqrt(var + 1e-06) * norm_gain[0]).astype(jnp.bfloat16)
    scores = jax.nn.sigmoid(jnp.dot(normed, router[0], preferred_element_type=jnp.float32))
    experts = jnp.arange(router.shape[2]).astype(jnp.float32)
    picked = jnp.sum((last_ids[:, :, None] == experts[None, None, :]).astype(jnp.float32), axis=1)
    weight = 2.5 * scores[:, 0] * picked[:, 0] / jnp.sum(scores * picked, axis=-1)

    both = lax.all_gather(after(normed, (arrived[0], packed[3])), "expert", axis=0, tiled=True)
    partials = expert_part(after(both, arrived[1]), w_gate[0], w_up[0], w_down[0])
    summed = lax.psum_scatter(after(partials, arrived[2]), "expert", scatter_dimension=0, tiled=True).astype(jnp.float32)
    is_kept = (jnp.arange(size) < count)[:, None]
    delta = jnp.where(is_kept, summed * weight[:, None], 0.0)
    updated = (last32 + delta).astype(jnp.bfloat16)

    moved_last = passed_along(updated, "section", 1)
    arrived.append(passed_along(after(packed[3], arrived[2]), "section", 1))

    out, before, start = None, None, 0
    for chunk, tiles in zip(arrived, CHUNKS):
        count = tiles + (start + tiles == 7)
        out = unpack(moved_pos, before, chunk, moved_last, out, start, count, start, rows, size)
        before, start = chunk, start + tiles
    return out[None]


def solution(mesh):
    return jax.shard_map(
        local,
        mesh=mesh,
        in_specs=(
            P("section", "expert", None),
            P("section", None),
            P("section", None, None),
            P("section", None, "expert"),
            P("section", None, "expert"),
            P("section", "expert", None),
            P(None, "section", "expert", None),
        ),
        out_specs=P("section", "expert", None),
        check_vma=False,
    )
```

time: 249 us -> 219 us (0.88)
  waiting for transfers between devices: 175 us -> 131 us
  Pallas kernels: 0 us -> 42.8 us
  other arithmetic: 22.3 us -> 8.49 us
  matrix products: 23.5 us -> 12.9 us
  local copies, waits for them, and re-layouts: 12.5 us -> 2.59 us
  starting transfers between devices: 1.81 us -> 6.32 us
    pallas_call x0 -> x9, Pallas kernels: none -> 42.8 us  [the longest x4 21.2 us: unpack(): pl.pallas_call(functools.partial(unpack_kernel, first, start, end, before...]
    ppermute x1 -> x6, waiting for transfers between devices: 162 us -> 128 us  [passed_along(): lax.ppermute(x, axis, [(i, (i + by) % devices) for i in range(devices)])]
    all_gather x1, waiting for transfers between devices: 13 us -> 0.01 us  [local(): lax.all_gather(after(normed, (arrived[0], packed[3])), 'expert', axis=0,...]
    dot_general x4 -> x3, matrix products: 16.4 us -> 5.66 us  [the longest x1 3.69 us: expert_part(): upper = jnp.dot(piece, up_dev, preferred_element_type=jnp.float32)]
    gather x1 -> x0, local copies, waits for them, and re-layouts: 8.87 us -> none  [place_rows(): taken = jnp.take(slot_rows, safe_slot, axis=0)]
    reduce_sum x3, other arithmetic: 11.2 us -> 3.16 us  [the longest x1 1.48 us: local(): count = jnp.minimum(jnp.sum(chosen), size)]
    convert_element_type x1 -> x3, other arithmetic: 9.21 us -> 4.29 us  [the longest x1 2.4 us: local(): (last32 * lax.rsqrt(var + 1e-06) * norm_gain[0]).astype(jnp.bfloat16)]
    ppermute x1 -> x6, starting transfers between devices: 1.77 us -> 6.28 us  [passed_along(): lax.ppermute(x, axis, [(i, (i + by) % devices) for i in range(devices)])]
  transfers between devices with their start and end apart: 3 -> 8, of which waited for: 2 -> 5; matrix products, arithmetic and copies ran while one was open for 5% -> 9% of each run, Pallas kernels for 0% -> 14%
where the time goes in v1:
time: 219 us
  waiting for transfers between devices  131 us (60%)
  Pallas kernels  42.8 us (20%)
  between operations  14.2 us (6%)
  matrix products  12.9 us (6%)
  other arithmetic  8.49 us (4%)
  starting transfers between devices  6.32 us (3%)
  local copies, waits for them, and re-layouts  2.59 us (1%)
    ppermute x6, waiting for transfers between devices, passed_along(): lax.ppermute(x, axis, [(i, (i + by) % devices) for i in range(devices)])  128 us
    pallas_call x4, Pallas kernels, unpack(): pl.pallas_call(functools.partial(unpack_kernel, first, start, end, before...  21.2 us
    pallas_call x4, Pallas kernels, pack(): pl.pallas_call(functools.partial(pack_kernel, first), grid=(tiles,), in_s...  15.7 us
    dot_general x1, matrix products, expert_part(): partial_out = jnp.dot(active, down_dev, preferred_element_type=jnp.float32)  7.26 us
    ppermute x6, starting transfers between devices, passed_along(): lax.ppermute(x, axis, [(i, (i + by) % devices) for i in range(devices)])  6.28 us
    pallas_call x1, Pallas kernels, pack_last(): pl.pallas_call(functools.partial(pack_last_kernel, base), grid=(rows // s...  5.91 us
  transfers between devices with their start and end apart: 8, of which 5 were waited for; matrix products, arithmetic and copies ran while one was open for 9% of the time, Pallas kernels for 14%

profile of v1, /device:TPU:0, one launch (start us, length us, event | category | flops | bytes accessed | tf_op | source)
XLA Modules:
  0.0 218.6 jit_solution(8957342254899488377)
XLA Ops:
  6.5 0.0 copy-start
  6.5 0.0 all-gather.2.cloned.1.call-start
  6.5 1.5 convert_reduce_fusion.1
  8.0 0.3 reduce-window.9
  8.3 0.1 slice.13
  8.4 0.1 slice_reduce_fusion
  9.2 0.1 fusion.25
  9.3 0.6 and_select_fusion.pos_a.pos_b.pos
  9.9 3.0 %pack_rows.5 = bf16[128,3584]{1,0:T(8,128)(2,1)} custom-call(s32[1,1024]{1,0:T(1,128)} %and_select_fusion.pos_a.pos_b.pos, s32[1,1024]{1,0:T(1,128)} %and_select_fusion.pos_a.pos_b.pos, bf16[1024,3584]{1,0:T(8,128)(2,1)} %bitcast.39, bf16[1024,3584]{1,0:T(8,128)(2,1)} %bitcast.40), custom_call_target="tpu_custom_call" | custom-call | flops 234881024 | bytes 1835008 | tf_op jit(solution)/shard_map/pack_rows/pallas_call | solution.py:39
  12.9 2.9 %collective-permute-start.1 = (bf16[128,3584]{1,0:T(8,128)(2,1)}, bf16[128,3584]{1,0:T(8,128)(2,1)S(1)}, u32[]{:S(2)}, u32[]{:S(2)}) collective-permute-start(bf16[128,3584]{1,0:T(8,128)(2,1)} %pack_rows.5), channel_id=1, source_target_pairs={{0,2},{2,4},{4,6},{6,8},{8,10},{10,12},{12,14},{14,16},{16,18},{18... | collective-permute-start | bytes 2752520 | tf_op jit(solution)/shard_map/ppermute | solution.py:17
  15.8 3.0 %pack_rows.7 = bf16[128,3584]{1,0:T(8,128)(2,1)} custom-call(s32[1,1024]{1,0:T(1,128)} %and_select_fusion.pos_a.pos_b.pos, s32[1,1024]{1,0:T(1,128)} %and_select_fusion.pos_a.pos_b.pos, bf16[1024,3584]{1,0:T(8,128)(2,1)} %bitcast.41, bf16[1024,3584]{1,0:T(8,128)(2,1)} %bitcast.42), custom_call_target="tpu_custom_call" | custom-call | flops 234881024 | bytes 1835008 | tf_op jit(solution)/shard_map/pack_rows/pallas_call | solution.py:39
  18.8 5.9 %pack_rows.6 = bf16[384,3584]{1,0:T(8,128)(2,1)} custom-call(s32[1,1024]{1,0:T(1,128)} %and_select_fusion.pos_a.pos_b.pos, s32[1,1024]{1,0:T(1,128)} %and_select_fusion.pos_a.pos_b.pos, bf16[1024,3584]{1,0:T(8,128)(2,1)} %bitcast.43, bf16[1024,3584]{1,0:T(8,128)(2,1)} %bitcast.44), custom_call_target="tpu_custom_call" | custom-call | flops 704643072 | bytes 5505024 | tf_op jit(solution)/shard_map/pack_rows/pallas_call | solution.py:39
  24.7 0.0 copy-start.7
  24.7 5.9 %pack_last.1 = bf16[128,3584]{1,0:T(8,128)(2,1)} custom-call(s32[1,1024]{1,0:T(1,128)} %and_select_fusion.pos_a.pos_b.pos, bf16[1024,3584]{1,0:T(8,128)(2,1)} %bitcast.45), custom_call_target="tpu_custom_call" | custom-call | flops 939524096 | bytes 7340032 | tf_op jit(solution)/shard_map/pack_last/pallas_call | solution.py:78
  30.6 1.4 fusion.5
  32.1 0.0 copy-done.7
  32.1 2.4 %fusion.7 = bf16[128,3584]{1,0:T(8,128)(2,1)} fusion(bf16[128,3584]{1,0:T(8,128)(2,1)} %pack_last.1, f32[3584]{0:T(1024)S(1)} %reduce.4, f32[128]{0:T(128)S(1)} %add_rsqrt_fusion), kind=kLoop, calls=%fused_computation.11 | loop fusion | flops 1835008 | bytes 1849856 | tf_op jit(solution)/shard_map/convert_element_type | solution.py:195
  34.5 5.8 %collective-permute-done.1.refs_1_.refs_2_ = bf16[128,3584]{1,0:T(8,128)(2,1)S(1)} collective-permute-done((bf16[128,3584]{1,0:T(8,128)(2,1)}, bf16[128,3584]{1,0:T(8,128)(2,1)S(1)}, u32[]{:S(2)}, u32[]{:S(2)}) %collective-permute-start.1) | collective-permute-done | bytes 917536 | tf_op jit(solution)/shard_map/ppermute | solution.py:17
  40.4 0.0 copy-start.3
  40.4 0.0 all-gather.2.cloned.1.call-update
  40.4 0.0 reduce-scatter.2.cloned.1.call-start
  40.4 0.1 collective-permute-start.4
  40.5 0.8 copy-done.3
  41.3 3.8 %pack_rows.4 = bf16[256,3584]{1,0:T(8,128)(2,1)} custom-call(s32[1,1024]{1,0:T(1,128)} %and_select_fusion.pos_a.pos_b.pos, s32[1,1024]{1,0:T(1,128)} %and_select_fusion.pos_a.pos_b.pos, bf16[1024,3584]{1,0:T(8,128)(2,1)} %bitcast.46, bf16[1024,3584]{1,0:T(8,128)(2,1)} %bitcast.47), custom_call_target="tpu_custom_call" | custom-call | flops 469762048 | bytes 3670016 | tf_op jit(solution)/shard_map/pack_rows/pallas_call | solution.py:39
  45.1 0.0 collective-permute-start.2
  45.1 22.6 %collective-permute-done.4.refs_2_.refs_3_.refs_1_ = bf16[128,3584]{1,0:T(8,128)(2,1)} collective-permute-done((bf16[128,3584]{1,0:T(8,128)(2,1)}, bf16[128,3584]{1,0:T(8,128)(2,1)}, u32[]{:S(2)}, u32[]{:S(2)}) %collective-permute-start.4) | collective-permute-done | bytes 917536 | tf_op jit(solution)/shard_map/ppermute | solution.py:17
  67.7 0.0 all-gather.2.cloned.1.call-done
  67.7 3.7 %fusion.1 = f32[256,512]{1,0:T(8,128)S(1)} fusion(bf16[256,3584]{1,0:T(8,128)(2,1)} %all-gather.2.cloned.1.call-done, bf16[1,3584,512]{2,1,0:T(8,128)(2,1)} %param.11), kind=kOutput, calls=%fused_computation.2 | convolution fusion | flops 939524096 | bytes 6029312 | tf_op jit(solution)/shard_map/dot_general | solution.py:157
  71.4 7.3 %convolution_convert_fusion = bf16[256,3584]{1,0:T(8,128)(2,1)} fusion(bf16[1,512,3584]{2,1,0:T(8,128)(2,1)} %param.12, f32[256,512]{1,0:T(8,128)S(1)} %fusion.1, bf16[256,3584]{1,0:T(8,128)(2,1)} %all-gather.2.cloned.1.call-done, bf16[1,3584,512]{2,1,0:T(8,128)(2,1)} %param.10), kind=kOutput, calls=%fused_computation | convolution fusion | flops 1880752128 | bytes 11534336 | tf_op jit(solution)/shard_map/dot_general | solution.py:159
  78.6 0.0 copy-start.6
  78.7 26.5 %collective-permute-done.2.refs_2_.refs_3_.refs_1_ = bf16[256,3584]{1,0:T(8,128)(2,1)S(1)} collective-permute-done((bf16[256,3584]{1,0:T(8,128)(2,1)}, bf16[256,3584]{1,0:T(8,128)(2,1)S(1)}, u32[]{:S(2)}, u32[]{:S(2)}) %collective-permute-start.2) | collective-permute-done | bytes 1835040 | tf_op jit(solution)/shard_map/ppermute | solution.py:17
  105.2 0.0 copy-start.1
  105.2 0.0 reduce-scatter.2.cloned.1.call-update
  105.2 0.0 copy-done.6
  105.2 0.3 fusion.17
  105.5 0.1 collective-permute-start.3
  105.5 0.2 convert_reduce_fusion
  105.8 0.1 copy.14
  105.9 0.0 copy-done
  105.9 1.7 multiply_reduce_fusion
  107.6 0.0 copy-done.1
  107.6 0.0 copy-start.4
  107.6 2.9 %reduce-scatter.2.cloned.1.call-done = bf16[128,3584]{1,0:T(8,128)(2,1)} async-done(((bf16[256,3584]{1,0:T(8,128)(2,1)}), bf16[128,3584]{1,0:T(8,128)(2,1)}) %reduce-scatter.2.cloned.1.call-update) | async-done | bytes 917520 | tf_op jit(solution)/shard_map/reduce_scatter | solution.py:203
  110.6 1.9 fusion.8
  112.5 1.8 collective-permute-start.5
  114.2 0.0 copy-done.4
  114.2 1.5 collective-permute-start
  115.7 73.3 %collective-permute-done.refs_0_ = s32[1,1024]{1,0:T(1,128)S(1)} collective-permute-done((s32[1,1024]{1,0:T(1,128)S(1)}, s32[1,1024]{1,0:T(1,128)S(1)}, u32[]{:S(2)}, u32[]{:S(2)}) %collective-permute-start) | collective-permute-done | bytes 4128 | tf_op jit(solution)/shard_map/ppermute | solution.py:17
  189.0 0.0 copy-start.5
  189.0 0.0 collective-permute-done.5.refs_3_.refs_4_
  189.0 0.6 copy-done.5
  189.6 0.0 copy-start.2
  189.6 0.9 copy-done.2
  190.5 3.6 %unpack_rows.4.refs_5_ = bf16[1024,3584]{1,0:T(8,128)(2,1)} custom-call(s32[1,1024]{1,0:T(1,128)} %copy-done.5, bf16[128,3584]{1,0:T(8,128)(2,1)} %copy-done.3, bf16[128,3584]{1,0:T(8,128)(2,1)} %copy-done.3, bf16[128,3584]{1,0:T(8,128)(2,1)} %copy-done.2), custom_call_target="tpu_custom_call" | custom-call | flops 352321536 | bytes 2752512 | tf_op jit(solution)/shard_map/unpack_rows/pallas_call | solution.py:140
  194.1 4.1 %unpack_rows.5.refs_5_ = bf16[1024,3584]{1,0:T(8,128)(2,1)} custom-call(s32[1,1024]{1,0:T(1,128)} %copy-done.5, bf16[128,3584]{1,0:T(8,128)(2,1)} %copy-done.3, bf16[128,3584]{1,0:T(8,128)(2,1)} %collective-permute-done.4.refs_2_.refs_3_.refs_1_, bf16[128,3584]{1,0:T(8,128)(2,1)} %collective-permute-done.4.refs_2_.refs_3_.refs_1_, ...), custom_call_target="tpu_custom_call", output_to_operand_aliasing={{}: (5, {})} | custom-call | flops 352321536 | bytes 2752512 | tf_op jit(solution)/shard_map/unpack_rows/pallas_call | solution.py:140
  198.2 5.4 %unpack_rows.6.refs_5_ = bf16[1024,3584]{1,0:T(8,128)(2,1)} custom-call(s32[1,1024]{1,0:T(1,128)} %copy-done.5, bf16[128,3584]{1,0:T(8,128)(2,1)} %collective-permute-done.4.refs_2_.refs_3_.refs_1_, bf16[256,3584]{1,0:T(8,128)(2,1)} %copy-done.1, bf16[256,3584]{1,0:T(8,128)(2,1)} %copy-done.1, ...), custom_call_target="tpu_custom_call", output_to_operand_aliasing={{}: (5, {})} | custom-call | flops 704643072 | bytes 5505024 | tf_op jit(solution)/shard_map/unpack_rows/pallas_call | solution.py:140
  203.5 0.0 collective-permute-done.3.refs_2_.refs_3_
  203.5 8.2 %unpack_rows.7 = bf16[1024,3584]{1,0:T(8,128)(2,1)} custom-call(s32[1,1024]{1,0:T(1,128)} %copy-done.5, bf16[256,3584]{1,0:T(8,128)(2,1)} %copy-done.1, bf16[384,3584]{1,0:T(8,128)(2,1)} %collective-permute-done.3.refs_2_.refs_3_, bf16[384,3584]{1,0:T(8,128)(2,1)} %collective-permute-done.3.refs_2_.refs_3_, ...), custom_call_target="tpu_custom_call", output_to_operand_aliasing={{}: (5, {})} | custom-call | flops 1409286144 | bytes 11010048 | tf_op jit(solution)/shard_map/unpack_rows/pallas_call | solution.py:140
  (7 shorter events, 0.1 us)
Async XLA Ops:
  6.5 99.4 %copy-start = (bf16[1,3584,128]{2,1,0:T(8,128)(2,1)S(1)}, bf16[1,3584,128]{2,1,0:T(8,128)(2,1)}, u32[]{:S(2)}) copy-start(bf16[1,3584,128]{2,1,0:T(8,128)(2,1)} %param.9) | copy-start | bytes 2752516
  6.5 61.1 %all-gather.2.cloned.1.call-start = ((), (), s32[]{:S(2)}) async-start(), calls=%async_computation.1 | async-start | bytes 2752512 | tf_op jit(solution)/shard_map/all_gather | solution.py:201
  12.9 27.5 %collective-permute-start.1 = (bf16[128,3584]{1,0:T(8,128)(2,1)}, bf16[128,3584]{1,0:T(8,128)(2,1)S(1)}, u32[]{:S(2)}, u32[]{:S(2)}) collective-permute-start(bf16[128,3584]{1,0:T(8,128)(2,1)} %pack_rows.5), channel_id=1, source_target_pairs={{0,2},{2,4},{4,6},{6,8},{8,10},{10,12},{12,14},{14,16},{16,18},{18... | collective-permute-start | bytes 2752520 | tf_op jit(solution)/shard_map/ppermute | solution.py:17
  24.7 7.4 %copy-start.7 = (f32[1,3584]{1,0:T(1,128)S(1)}, f32[1,3584]{1,0:T(1,128)}, u32[]{:S(2)}) copy-start(f32[1,3584]{1,0:T(1,128)} %param.8) | copy-start | bytes 43012
  40.4 0.9 copy-start.3
  40.4 70.2 %reduce-scatter.2.cloned.1.call-start = ((), (), s32[]{:S(2)}) async-start(), calls=%async_computation.2 | async-start | bytes 2752512 | tf_op jit(solution)/shard_map/reduce_scatter | solution.py:203
  40.4 27.3 %collective-permute-start.4 = (bf16[128,3584]{1,0:T(8,128)(2,1)}, bf16[128,3584]{1,0:T(8,128)(2,1)}, u32[]{:S(2)}, u32[]{:S(2)}) collective-permute-start(bf16[128,3584]{1,0:T(8,128)(2,1)} %pack_rows.7), channel_id=1, source_target_pairs={{0,2},{2,4},{4,6},{6,8},{8,10},{10,12},{12,14},{14,16},{16,18},{18... | collective-permute-start | bytes 2752520 | tf_op jit(solution)/shard_map/ppermute | solution.py:17
  45.1 60.1 %collective-permute-start.2 = (bf16[256,3584]{1,0:T(8,128)(2,1)}, bf16[256,3584]{1,0:T(8,128)(2,1)S(1)}, u32[]{:S(2)}, u32[]{:S(2)}) collective-permute-start(bf16[256,3584]{1,0:T(8,128)(2,1)} %pack_rows.4), channel_id=1, source_target_pairs={{0,2},{2,4},{4,6},{6,8},{8,10},{10,12},{12,14},{14,16},{16,18},{18... | collective-permute-start | bytes 5505032 | tf_op jit(solution)/shard_map/ppermute | solution.py:17
  78.6 26.6 %copy-start.6 = (s32[1,1,1024,8]{2,3,1,0:T(8,128)S(1)}, s32[1,1,1024,8]{2,3,1,0:T(8,128)}, u32[]{:S(2)}) copy-start(s32[1,1,1024,8]{2,3,1,0:T(8,128)} %param.13) | copy-start | bytes 98308
  105.2 2.5 %copy-start.1 = (bf16[256,3584]{1,0:T(8,128)(2,1)}, bf16[256,3584]{1,0:T(8,128)(2,1)S(1)}, u32[]{:S(2)}) copy-start(bf16[256,3584]{1,0:T(8,128)(2,1)S(1)} %collective-permute-done.2.refs_2_.refs_3_.refs_1_) | copy-start | bytes 5505028
  105.5 98.1 %collective-permute-start.3 = (bf16[384,3584]{1,0:T(8,128)(2,1)}, bf16[384,3584]{1,0:T(8,128)(2,1)}, u32[]{:S(2)}, u32[]{:S(2)}) collective-permute-start(bf16[384,3584]{1,0:T(8,128)(2,1)} %pack_rows.6), channel_id=1, source_target_pairs={{0,2},{2,4},{4,6},{6,8},{8,10},{10,12},{12,14},{14,16},{16,18},{18... | collective-permute-start | bytes 8257544 | tf_op jit(solution)/shard_map/ppermute | solution.py:17
  107.6 6.6 %copy-start.4 = (s32[1,1024]{1,0:T(1,128)S(1)}, s32[1,1024]{1,0:T(1,128)}, u32[]{:S(2)}) copy-start(s32[1,1024]{1,0:T(1,128)} %and_select_fusion.pos_a.pos_b.pos) | copy-start | bytes 12292
  112.5 76.6 %collective-permute-start.5 = (bf16[128,3584]{1,0:T(8,128)(2,1)S(1)}, bf16[128,3584]{1,0:T(8,128)(2,1)S(1)}, u32[]{:S(2)}, u32[]{:S(2)}) collective-permute-start(bf16[128,3584]{1,0:T(8,128)(2,1)S(1)} %fusion.8), channel_id=1, source_target_pairs={{0,2},{2,4},{4,6},{6,8},{8,10},{10,12},{12,14},{14,16},{16,18},{18... | collective-permute-start | bytes 2752520 | tf_op jit(solution)/shard_map/ppermute | solution.py:17
  114.2 74.8 %collective-permute-start = (s32[1,1024]{1,0:T(1,128)S(1)}, s32[1,1024]{1,0:T(1,128)S(1)}, u32[]{:S(2)}, u32[]{:S(2)}) collective-permute-start(s32[1,1024]{1,0:T(1,128)S(1)} %copy-done.4), channel_id=1, source_target_pairs={{0,2},{2,4},{4,6},{6,8},{8,10},{10,12},{12,14},{14,16},{16,18},{18... | collective-permute-start | bytes 12296 | tf_op jit(solution)/shard_map/ppermute | solution.py:17
  189.0 0.6 copy-start.5
  189.6 0.9 copy-start.2
Sparse Core Ops, SparseCore 0:
  40.5 7.7 all-gather.1
  105.3 5.2 reduce-scatter.1

commit v2 on v1

v2 whole, which is shorter than its diff:
```python
import functools

import jax
import jax.numpy as jnp
from jax import lax
from jax.experimental import pallas as pl
from jax.experimental.pallas import tpu as pltpu
from jax.sharding import PartitionSpec as P

VMEM_LIMIT = 56 * 1024 * 1024
COLUMN_PARTS = 4
NOWHERE = -(1 << 20)
CHUNKS = (1, 5, 1)
LATER_COST = pl.CostEstimate(flops=1024, bytes_accessed=100000000, transcendentals=0)
SMALL_COST = pl.CostEstimate(flops=1024, bytes_accessed=1024, transcendentals=0)


def passed_along(x, axis, by):
    devices = lax.axis_size(axis)
    return lax.ppermute(x, axis, [(i, (i + by) % devices) for i in range(devices)])


def after(x, done):
    return lax.optimization_barrier((x, done))[0]


def onehot_to(pos, base, size):
    places = lax.broadcasted_iota(jnp.int32, (size, pos.shape[1]), 0) + base
    return jnp.where(places == pos, 1.0, 0.0).astype(jnp.bfloat16)


def pack_kernel(first, pos_a, pos_b, rows_a, rows_b, *refs):
    out = refs[-1]
    size = rows_a.shape[0]
    base = (pl.program_id(0) + first) * size
    onehot = onehot_to(jnp.concatenate([pos_a[...], pos_b[...]], axis=1), base, size)
    rows = jnp.concatenate([rows_a[...], rows_b[...]], axis=0)
    out[:size] = jnp.dot(onehot, rows, preferred_element_type=jnp.float32).astype(out.dtype)
    if len(refs) > 1:
        out[size:] = refs[0][...]


def pack(h, pos, first, tiles, size, cost=SMALL_COST, extra=None):
    width = h.shape[1]
    part = width // COLUMN_PARTS
    more = 0 if extra is None else extra.shape[0]
    assert tiles == 1 or not more
    specs = [
        pl.BlockSpec((1, size), lambda i, j: (0, i + first)),
        pl.BlockSpec((1, size), lambda i, j: (0, i + first + 1)),
        pl.BlockSpec((size, part), lambda i, j: (i + first, j)),
        pl.BlockSpec((size, part), lambda i, j: (i + first + 1, j)),
    ]
    args = [pos, pos, h, h]
    if more:
        specs.append(pl.BlockSpec((more, part), lambda i, j: (0, j)))
        args.append(extra)
    return pl.pallas_call(
        functools.partial(pack_kernel, first),
        grid=(tiles, COLUMN_PARTS),
        in_specs=specs,
        out_specs=pl.BlockSpec((size + more, part), lambda i, j: (i, j)),
        out_shape=jax.ShapeDtypeStruct((tiles * size + more, width), h.dtype),
        compiler_params=pltpu.CompilerParams(vmem_limit_bytes=VMEM_LIMIT),
        cost_estimate=cost,
        name="pack_rows",
    )(*args)


def pack_last_kernel(base, pos, rows, out, total):
    step = pl.program_id(0)
    part = jnp.dot(onehot_to(pos[...], base, out.shape[0]), rows[...], preferred_element_type=jnp.float32)

    @pl.when(step == 0)
    def _():
        total[...] = part

    @pl.when(step > 0)
    def _():
        total[...] += part

    @pl.when(step == pl.num_programs(0) - 1)
    def _():
        out[...] = total[...].astype(out.dtype)


def pack_last(h, pos, base, size):
    rows, width = h.shape
    step = 2 * size
    return pl.pallas_call(
        functools.partial(pack_last_kernel, base),
        grid=(rows // step,),
        in_specs=[
            pl.BlockSpec((1, step), lambda i: (0, i)),
            pl.BlockSpec((step, width), lambda i: (i, 0)),
        ],
        out_specs=pl.BlockSpec((size, width), lambda i: (0, 0)),
        out_shape=jax.ShapeDtypeStruct((size, width), h.dtype),
        scratch_shapes=[pltpu.VMEM((size, width), jnp.float32)],
        compiler_params=pltpu.CompilerParams(vmem_limit_bytes=VMEM_LIMIT),
        cost_estimate=SMALL_COST,
        name="pack_last",
    )(pos, h)


def unpack_kernel(first, windows, aliased, *refs):
    pos, last = refs[0], refs[1]
    sources = refs[2 : 2 + len(windows)]
    out, onehot = refs[2 + len(windows) + aliased :]
    size = last.shape[0]
    tile = pl.program_id(0) * 2 + first

    @pl.when(pl.program_id(1) == 0)
    def _():
        parts = [onehot_to(pos[...], 7 * size, size)]
        for offset, start, end in windows:
            place = tile + offset
            inside = (place >= start) & (place < end)
            parts.append(onehot_to(pos[...], jnp.where(inside, place, NOWHERE) * size, size))
        both = jnp.concatenate([part.astype(jnp.float32) for part in parts], axis=0)
        onehot[...] = both.T.astype(jnp.bfloat16)

    rows = jnp.concatenate([last[...]] + [ref[...] for ref in sources], axis=0)
    out[...] = jnp.dot(onehot[...], rows, preferred_element_type=jnp.float32).astype(out.dtype)


def unpack(pos, pieces, last, out, first, pairs, rows):
    size, width = last.shape
    part = width // COLUMN_PARTS
    specs = [
        pl.BlockSpec((1, 2 * size), lambda i, j: (0, i + first // 2)),
        pl.BlockSpec((size, part), lambda i, j: (0, j)),
    ]
    args = [pos, last]
    windows = []
    for piece, start in pieces:
        count = piece.shape[0] // size
        for offset in (-1, 0, 1):
            places = [first + 2 * pair + offset - start for pair in range(pairs)]
            if any(0 <= place < count for place in places):
                windows.append((offset, start, start + count))
                specs.append(
                    pl.BlockSpec(
                        (size, part),
                        lambda i, j, shift=first + offset - start, count=count: (
                            jnp.clip(2 * i + shift, 0, count - 1),
                            j,
                        ),
                    )
                )
                args.append(piece)
    aliases = {}
    if out is not None:
        aliases = {len(args): 0}
        specs.append(pl.BlockSpec(memory_space=pl.ANY))
        args.append(out)
    depth = size * (len(windows) + 1)
    return pl.pallas_call(
        functools.partial(unpack_kernel, first, tuple(windows), out is not None),
        grid=(pairs, COLUMN_PARTS),
        in_specs=specs,
        out_specs=pl.BlockSpec((2 * size, part), lambda i, j: (i + first // 2, j)),
        out_shape=jax.ShapeDtypeStruct((rows, width), last.dtype),
        scratch_shapes=[pltpu.VMEM((2 * size, depth), jnp.bfloat16)],
        input_output_aliases=aliases,
        compiler_params=pltpu.CompilerParams(vmem_limit_bytes=VMEM_LIMIT),
        cost_estimate=SMALL_COST,
        name="unpack_rows",
    )(*args)


def expert_rows(rows, gate_dev, up_dev, down_dev, out):
    gate = jnp.dot(rows[...], gate_dev[0], preferred_element_type=jnp.float32)
    upper = jnp.dot(rows[...], up_dev[0], preferred_element_type=jnp.float32)
    active = (jax.nn.silu(gate) * upper).astype(jnp.bfloat16)
    part = out.shape[1] // COLUMN_PARTS
    for j in range(COLUMN_PARTS):
        columns = slice(j * part, (j + 1) * part)
        out[:, columns] = jnp.dot(
            active, down_dev[0, :, columns], preferred_element_type=jnp.float32
        ).astype(out.dtype)


def update_kernel(
    last, picked, keep, gain, router, gate_dev, up_dev, down_dev, out,
    normed, normed_got, own_part, sent_part, got_part, sems,
):
    other = 1 - lax.axis_index("expert")
    barrier = pltpu.get_barrier_semaphore()
    pl.semaphore_signal(barrier, inc=1, device_id={"expert": other}, device_id_type=pl.DeviceIdType.MESH)

    last32 = last[...].astype(jnp.float32)
    var = jnp.mean(last32 * last32, axis=-1, keepdims=True)
    normed[...] = (last32 * lax.rsqrt(var + 1e-06) * gain[...]).astype(normed.dtype)
    pl.semaphore_wait(barrier, 1)
    rows_copy = pltpu.make_async_remote_copy(
        src_ref=normed, dst_ref=normed_got, send_sem=sems.at[0], recv_sem=sems.at[1],
        device_id={"expert": other}, device_id_type=pl.DeviceIdType.MESH,
    )
    rows_copy.start()

    scores = jax.nn.sigmoid(jnp.dot(normed[...], router[0], preferred_element_type=jnp.float32))
    named = scores * picked[...]
    weight = 2.5 * named[:, 0:1] / jnp.sum(named, axis=-1, keepdims=True)
    expert_rows(normed, gate_dev, up_dev, down_dev, own_part)

    rows_copy.wait()
    expert_rows(normed_got, gate_dev, up_dev, down_dev, sent_part)
    part_copy = pltpu.make_async_remote_copy(
        src_ref=sent_part, dst_ref=got_part, send_sem=sems.at[2], recv_sem=sems.at[3],
        device_id={"expert": other}, device_id_type=pl.DeviceIdType.MESH,
    )
    part_copy.start()
    part_copy.wait()
    summed = own_part[...].astype(jnp.float32) + got_part[...].astype(jnp.float32)
    delta = jnp.where(keep[...] > 0.0, summed * weight, 0.0)
    out[...] = (last[...].astype(jnp.float32) + delta).astype(out.dtype)


def update(last, picked, keep, norm_gain, router, w_gate, w_up, w_down):
    block = pltpu.VMEM(last.shape, last.dtype)
    return pl.pallas_call(
        update_kernel,
        in_specs=[pl.BlockSpec(memory_space=pltpu.VMEM)] * 8,
        out_specs=pl.BlockSpec(memory_space=pltpu.VMEM),
        out_shape=jax.ShapeDtypeStruct(last.shape, last.dtype),
        scratch_shapes=[block] * 5 + [pltpu.SemaphoreType.DMA((4,))],
        compiler_params=pltpu.CompilerParams(
            collective_id=0, has_side_effects=True, vmem_limit_bytes=VMEM_LIMIT
        ),
        cost_estimate=SMALL_COST,
        name="expert_update",
    )(last, picked, keep, norm_gain, router, w_gate, w_up, w_down)


def local(state, norm_gain, router, w_gate, w_up, w_down, route_ids):
    h = state[0]
    rows = h.shape[0]
    size = rows // 8
    raw_rows = rows - size
    ids = route_ids[0, 0]

    chosen = jnp.sum((ids == 0).astype(jnp.int32), axis=-1)
    slot = jnp.cumsum(chosen) - chosen
    kept = (chosen > 0) & (slot < size)
    count = jnp.minimum(jnp.sum(chosen), size)
    other = jnp.arange(rows, dtype=jnp.int32) - jnp.minimum(slot, size)
    pos = jnp.where(kept, raw_rows + slot, jnp.where(other < raw_rows, other, other + count))
    pos = pos.astype(jnp.int32)[None, :]

    places = jnp.concatenate([pos // 256, pos % 256], axis=1).astype(h.dtype)
    extra = jnp.pad(places, ((0, 15), (0, h.shape[1] - 2 * rows)))
    packed = [pack(h, pos, 0, CHUNKS[0], size, extra=extra)]
    packed.append(pack(h, after(pos, packed), CHUNKS[0], CHUNKS[1], size))
    moved = [passed_along(packed[0], "section", 1), passed_along(packed[1], "section", 1)]
    start = CHUNKS[0] + CHUNKS[1]
    packed.append(pack(h, after(pos, moved[0]), start, CHUNKS[2], size, LATER_COST))
    moved.append(passed_along(after(packed[2], moved[1]), "section", 1))
    places = moved[0][size].astype(jnp.int32)
    moved_pos = (places[:rows] * 256 + places[rows : 2 * rows])[None, :]
    last = pack_last(h, after(pos, packed[:2]), raw_rows, size)

    last_ids = jnp.dot(
        onehot_to(pos, raw_rows, size), ids.astype(jnp.bfloat16), preferred_element_type=jnp.float32
    )
    experts = jnp.arange(router.shape[2]).astype(jnp.float32)
    picked = jnp.sum((last_ids[:, :, None] == experts[None, None, :]).astype(jnp.float32), axis=1)
    keep = (jnp.arange(size) < count).astype(jnp.float32)[:, None]
    updated = update(last, picked, keep, norm_gain, router, w_gate, w_up, w_down)
    moved_last = passed_along(updated, "section", 1)

    pieces = [(moved[0], 0), (moved[1], 1), (moved[2], 6)]
    out = unpack(moved_pos, pieces[:2], moved_last, None, 0, 3, rows)
    out = unpack(moved_pos, pieces[1:], moved_last, out, 6, 1, rows)
    return out[None]


def solution(mesh):
    return jax.shard_map(
        local,
        mesh=mesh,
        in_specs=(
            P("section", "expert", None),
            P("section", None),
            P("section", None, None),
            P("section", None, "expert"),
            P("section", None, "expert"),
            P("section", "expert", None),
            P(None, "section", "expert", None),
        ),
        out_specs=P("section", "expert", None),
        check_vma=False,
    )
```

time: 219 us -> 198 us (0.904)
  Pallas kernels: 42.8 us -> 62.4 us
  between operations: 14.2 us -> 0.73 us
  matrix products: 12.9 us -> 0.26 us
  waiting for transfers between devices: 131 us -> 120 us
  other arithmetic: 8.49 us -> 5.32 us
    pallas_call x8 -> x6, Pallas kernels: 36.9 us -> 56.5 us  [the longest x3 24 us: pack(): pl.pallas_call(functools.partial(pack_kernel, first), grid=(tiles, COLUMN...]
    dot_general x3 -> x0, matrix products: 12.7 us -> none  [the longest x1 7.26 us: expert_part(): partial_out = jnp.dot(active, down_dev, preferred_element_type=jnp.float32)]
    ppermute x6 -> x4, waiting for transfers between devices: 128 us -> 120 us  [passed_along(): lax.ppermute(x, axis, [(i, (i + by) % devices) for i in range(devices)])]
    convert_element_type x2, other arithmetic: 4.28 us -> 0.66 us  [the longest x1 0.64 us: local(): keep = (jnp.arange(size) < count).astype(jnp.float32)[:, None]]
    reduce_scatter x1 -> x0, waiting for transfers between devices: 2.93 us -> none  [local(): lax.psum_scatter(after(partials, arrived[2]), 'expert', scatter_dimension...]
    ppermute x6 -> x4, starting transfers between devices: 6.28 us -> 6.04 us  [passed_along(): lax.ppermute(x, axis, [(i, (i + by) % devices) for i in range(devices)])]
  transfers between devices with their start and end apart: 8 -> 4, of which waited for: 5 -> 3; matrix products, arithmetic and copies ran while one was open for 9% -> 1% of each run, Pallas kernels for 14% -> 19%
where the time goes in v2:
time: 198 us; the launch traced here: 197 us
  waiting for transfers between devices  120 us (61%)
  Pallas kernels  62.4 us (32%)
  starting transfers between devices  6.04 us (3%)
  other arithmetic  5.32 us (3%)
  local copies, waits for them, and re-layouts  2.09 us (1%)
    ppermute x4, waiting for transfers between devices, passed_along(): lax.ppermute(x, axis, [(i, (i + by) % devices) for i in range(devices)])  120 us
    pallas_call x3, Pallas kernels, pack(): pl.pallas_call(functools.partial(pack_kernel, first), grid=(tiles, COLUMN...  24 us
    pallas_call x2, Pallas kernels, unpack(): pl.pallas_call(functools.partial(unpack_kernel, first, tuple(windows), ou...  19 us
    pallas_call x1, Pallas kernels, update(): pl.pallas_call(update_kernel, in_specs=[pl.BlockSpec(memory_space=pltpu.V...  13.4 us
    ppermute x4, starting transfers between devices, passed_along(): lax.ppermute(x, axis, [(i, (i + by) % devices) for i in range(devices)])  6.04 us
    pallas_call x1, Pallas kernels, pack_last(): pl.pallas_call(functools.partial(pack_last_kernel, base), grid=(rows // s...  5.9 us
  transfers between devices with their start and end apart: 4, of which 3 were waited for; matrix products, arithmetic and copies ran while one was open for 1% of the time, Pallas kernels for 19%

profile of v2, /device:TPU:0, one launch (start us, length us, event | category | flops | bytes accessed | tf_op | source)
XLA Modules:
  0.0 196.9 jit_solution(3191049373395071930)
XLA Ops:
  0.0 1.4 convert_reduce_fusion.1
  1.4 0.3 reduce-window.9
  1.7 0.1 slice.18
  1.8 0.1 slice_reduce_fusion
  2.6 0.1 fusion.14
  2.7 0.6 and_select_fusion.pos_a.pos_b.pos
  3.3 0.7 fusion.10.refs_0_
  4.0 4.1 %pack_rows.3 = bf16[144,3584]{1,0:T(8,128)(2,1)} custom-call(s32[1,1024]{1,0:T(1,128)} %and_select_fusion.pos_a.pos_b.pos, s32[1,1024]{1,0:T(1,128)} %and_select_fusion.pos_a.pos_b.pos, bf16[1024,3584]{1,0:T(8,128)(2,1)} %bitcast.13, bf16[1024,3584]{1,0:T(8,128)(2,1)} %bitcast.14, bf16[16,3584]{1,0:T(8,128)(2,1)} %fusion.10.refs_0_), custom_call_target="tpu_custom_call" | custom-call | flops 1024 | bytes 1024 | tf_op jit(solution)/shard_map/pack_rows/pallas_call | solution.py:58
  8.0 0.0 copy-start.3
  8.0 15.6 %pack_rows.4 = bf16[640,3584]{1,0:T(8,128)(2,1)} custom-call(s32[1,1024]{1,0:T(1,128)} %and_select_fusion.pos_a.pos_b.pos, s32[1,1024]{1,0:T(1,128)} %and_select_fusion.pos_a.pos_b.pos, bf16[1024,3584]{1,0:T(8,128)(2,1)} %bitcast.15, bf16[1024,3584]{1,0:T(8,128)(2,1)} %bitcast.16), custom_call_target="tpu_custom_call" | custom-call | flops 1024 | bytes 1024 | tf_op jit(solution)/shard_map/pack_rows/pallas_call | solution.py:58
  23.6 0.0 copy-start.5
  23.6 3.0 %collective-permute-start.2 = (bf16[640,3584]{1,0:T(8,128)(2,1)}, bf16[640,3584]{1,0:T(8,128)(2,1)S(1)}, u32[]{:S(2)}, u32[]{:S(2)}) collective-permute-start(bf16[640,3584]{1,0:T(8,128)(2,1)} %pack_rows.4), channel_id=1, source_target_pairs={{0,2},{2,4},{4,6},{6,8},{8,10},{10,12},{12,14},{14,16},{16,18},{18... | collective-permute-start | bytes 13762568 | tf_op jit(solution)/shard_map/ppermute | solution.py:20
  26.5 0.0 copy-done.3
  26.5 1.5 collective-permute-start
  28.0 5.9 %pack_last.1.last = bf16[128,3584]{1,0:T(8,128)(2,1)} custom-call(s32[1,1024]{1,0:T(1,128)} %and_select_fusion.pos_a.pos_b.pos, bf16[1024,3584]{1,0:T(8,128)(2,1)} %bitcast.17), custom_call_target="tpu_custom_call" | custom-call | flops 1024 | bytes 1024 | tf_op jit(solution)/shard_map/pack_last/pallas_call | solution.py:90
  33.9 0.6 fusion.11.keep
  34.6 0.0 copy-done.5
  34.6 0.3 fusion
  34.8 0.8 convert_reduce_fusion.picked
  35.7 13.4 %expert_update.1 = bf16[128,3584]{1,0:T(8,128)(2,1)} custom-call(bf16[128,3584]{1,0:T(8,128)(2,1)} %pack_last.1.last, f32[128,128]{1,0:T(8,128)} %convert_reduce_fusion.picked, f32[128,1]{1,0:T(8,128)} %fusion.11.keep, f32[1,3584]{1,0:T(1,128)} %gain.1, bf16[1,3584,128]{2,1,0:T(8,128)(2,1)} %router.1, bf16[1,3584,512]{2,1,0:T(8,128)(2,1)} %gate_dev.1, ...), custom_call_target="tpu_custom_call" | custom-call | flops 1024 | bytes 1024 | tf_op jit(solution)/shard_map/expert_update/pallas_call | solution.py:222
  49.1 1.6 collective-permute-start.1
  50.7 102.0 %collective-permute-done.refs_2_ = bf16[144,3584]{1,0:T(8,128)(2,1)S(1)} collective-permute-done((bf16[144,3584]{1,0:T(8,128)(2,1)S(1)}, bf16[144,3584]{1,0:T(8,128)(2,1)S(1)}, u32[]{:S(2)}, u32[]{:S(2)}) %collective-permute-start) | collective-permute-done | bytes 1032224 | tf_op jit(solution)/shard_map/ppermute | solution.py:20
  152.7 0.0 copy-start.2
  152.7 4.4 %pack_rows.5 = bf16[128,3584]{1,0:T(8,128)(2,1)} custom-call(s32[1,1024]{1,0:T(1,128)} %and_select_fusion.pos_a.pos_b.pos, s32[1,1024]{1,0:T(1,128)} %and_select_fusion.pos_a.pos_b.pos, bf16[1024,3584]{1,0:T(8,128)(2,1)} %bitcast.18, bf16[1024,3584]{1,0:T(8,128)(2,1)} %bitcast.19), custom_call_target="tpu_custom_call" | custom-call | flops 1024 | bytes 100000000 | tf_op jit(solution)/shard_map/pack_rows/pallas_call | solution.py:58
  157.1 0.0 collective-permute-done.2.refs_3_.refs_4_.refs_5_.refs_2_
  157.1 0.0 copy-start
  157.1 0.1 collective-permute-start.3
  157.2 0.0 copy-done.2
  157.2 0.7 slice_add_fusion.refs_0_
  157.9 14.4 %collective-permute-done.1.refs_1_ = bf16[128,3584]{1,0:T(8,128)(2,1)S(1)} collective-permute-done((bf16[128,3584]{1,0:T(8,128)(2,1)}, bf16[128,3584]{1,0:T(8,128)(2,1)S(1)}, u32[]{:S(2)}, u32[]{:S(2)}) %collective-permute-start.1) | collective-permute-done | bytes 917536 | tf_op jit(solution)/shard_map/ppermute | solution.py:20
  172.3 0.0 copy-done
  172.3 0.0 copy-start.1
  172.3 0.9 copy-done.1
  173.3 14.2 %unpack_rows.2.refs_4_ = bf16[1024,3584]{1,0:T(8,128)(2,1)} custom-call(s32[1,1024]{1,0:T(1,128)} %slice_add_fusion.refs_0_, bf16[128,3584]{1,0:T(8,128)(2,1)} %copy-done.1, bf16[144,3584]{1,0:T(8,128)(2,1)} %copy-done.2, bf16[640,3584]{1,0:T(8,128)(2,1)} %copy-done, bf16[640,3584]{1,0:T(8,128)(2,1)} %copy-done, bf16[640,3584]{1,0:T(8,128)(2,1)} %copy-done), custom_call_target="tpu_custom_call" | custom-call | flops 1024 | bytes 1024 | tf_op jit(solution)/shard_map/unpack_rows/pallas_call | solution.py:158
  187.5 3.7 %collective-permute-done.3.refs_3_ = bf16[128,3584]{1,0:T(8,128)(2,1)S(1)} collective-permute-done((bf16[128,3584]{1,0:T(8,128)(2,1)}, bf16[128,3584]{1,0:T(8,128)(2,1)S(1)}, u32[]{:S(2)}, u32[]{:S(2)}) %collective-permute-start.3) | collective-permute-done | bytes 917536 | tf_op jit(solution)/shard_map/ppermute | solution.py:20
  191.2 0.0 copy-start.4
  191.2 0.9 copy-done.4
  192.1 4.8 %unpack_rows.3 = bf16[1024,3584]{1,0:T(8,128)(2,1)} custom-call(s32[1,1024]{1,0:T(1,128)} %slice_add_fusion.refs_0_, bf16[128,3584]{1,0:T(8,128)(2,1)} %copy-done.1, bf16[640,3584]{1,0:T(8,128)(2,1)} %copy-done, bf16[128,3584]{1,0:T(8,128)(2,1)} %copy-done.4, bf16[1024,3584]{1,0:T(8,128)(2,1)} %unpack_rows.2.refs_4_), custom_call_target="tpu_custom_call", output_to_operand_aliasing={{}: (4, {})} | custom-call | flops 1024 | bytes 1024 | tf_op jit(solution)/shard_map/unpack_rows/pallas_call | solution.py:158
  (7 shorter events, 0.1 us)
Async XLA Ops:
  8.0 18.5 %copy-start.3 = (bf16[144,3584]{1,0:T(8,128)(2,1)S(1)}, bf16[144,3584]{1,0:T(8,128)(2,1)}, u32[]{:S(2)}) copy-start(bf16[144,3584]{1,0:T(8,128)(2,1)} %pack_rows.3) | copy-start | bytes 3096580
  23.6 11.0 %copy-start.5 = (s32[1,1,1024,8]{2,3,1,0:T(8,128)S(1)}, s32[1,1,1024,8]{2,3,1,0:T(8,128)}, u32[]{:S(2)}) copy-start(s32[1,1,1024,8]{2,3,1,0:T(8,128)} %param.13) | copy-start | bytes 98308
  23.6 133.5 %collective-permute-start.2 = (bf16[640,3584]{1,0:T(8,128)(2,1)}, bf16[640,3584]{1,0:T(8,128)(2,1)S(1)}, u32[]{:S(2)}, u32[]{:S(2)}) collective-permute-start(bf16[640,3584]{1,0:T(8,128)(2,1)} %pack_rows.4), channel_id=1, source_target_pairs={{0,2},{2,4},{4,6},{6,8},{8,10},{10,12},{12,14},{14,16},{16,18},{18... | collective-permute-start | bytes 13762568 | tf_op jit(solution)/shard_map/ppermute | solution.py:20
  26.5 126.1 %collective-permute-start = (bf16[144,3584]{1,0:T(8,128)(2,1)S(1)}, bf16[144,3584]{1,0:T(8,128)(2,1)S(1)}, u32[]{:S(2)}, u32[]{:S(2)}) collective-permute-start(bf16[144,3584]{1,0:T(8,128)(2,1)S(1)} %copy-done.3), channel_id=1, source_target_pairs={{0,2},{2,4},{4,6},{6,8},{8,10},{10,12},{12,14},{14,16},{16,18},{18... | collective-permute-start | bytes 3096584 | tf_op jit(solution)/shard_map/ppermute | solution.py:20
  49.1 123.2 %collective-permute-start.1 = (bf16[128,3584]{1,0:T(8,128)(2,1)}, bf16[128,3584]{1,0:T(8,128)(2,1)S(1)}, u32[]{:S(2)}, u32[]{:S(2)}) collective-permute-start(bf16[128,3584]{1,0:T(8,128)(2,1)} %expert_update.1), channel_id=1, source_target_pairs={{0,2},{2,4},{4,6},{6,8},{8,10},{10,12},{12,14},{14,16},{16,18},{18... | collective-permute-start | bytes 2752520 | tf_op jit(solution)/shard_map/ppermute | solution.py:20
  152.7 4.5 %copy-start.2 = (bf16[144,3584]{1,0:T(8,128)(2,1)}, bf16[144,3584]{1,0:T(8,128)(2,1)S(1)}, u32[]{:S(2)}) copy-start(bf16[144,3584]{1,0:T(8,128)(2,1)S(1)} %collective-permute-done.refs_2_) | copy-start | bytes 3096580
  157.1 15.2 %copy-start = (bf16[640,3584]{1,0:T(8,128)(2,1)}, bf16[640,3584]{1,0:T(8,128)(2,1)S(1)}, u32[]{:S(2)}) copy-start(bf16[640,3584]{1,0:T(8,128)(2,1)S(1)} %collective-permute-done.2.refs_3_.refs_4_.refs_5_.refs_2_) | copy-start | bytes 13762564
  157.1 34.1 %collective-permute-start.3 = (bf16[128,3584]{1,0:T(8,128)(2,1)}, bf16[128,3584]{1,0:T(8,128)(2,1)S(1)}, u32[]{:S(2)}, u32[]{:S(2)}) collective-permute-start(bf16[128,3584]{1,0:T(8,128)(2,1)} %pack_rows.5), channel_id=1, source_target_pairs={{0,2},{2,4},{4,6},{6,8},{8,10},{10,12},{12,14},{14,16},{16,18},{18... | collective-permute-start | bytes 2752520 | tf_op jit(solution)/shard_map/ppermute | solution.py:20
  172.3 0.9 copy-start.1
  191.2 0.9 copy-start.4

commit v3 on v2

v3 whole, which is shorter than its diff:
```python
import functools

import jax
import jax.numpy as jnp
from jax import lax
from jax.experimental import pallas as pl
from jax.experimental.pallas import tpu as pltpu
from jax.sharding import PartitionSpec as P

VMEM_LIMIT = 56 * 1024 * 1024
COLUMN_PARTS = 4
EARLY = 3
SMALL_COST = pl.CostEstimate(flops=1024, bytes_accessed=1024, transcendentals=0)
PARAMS = pltpu.CompilerParams(vmem_limit_bytes=VMEM_LIMIT)


def passed_along(x, axis, by):
    devices = lax.axis_size(axis)
    return lax.ppermute(x, axis, [(i, (i + by) % devices) for i in range(devices)])


def after(x, done):
    return lax.optimization_barrier((x, done))[0]


def onehot_to(pos, base, size):
    places = lax.broadcasted_iota(jnp.int32, (size, pos.shape[1]), 0) + base
    return jnp.where(places == pos, 1.0, 0.0).astype(jnp.bfloat16)


def pack_kernel(base, with_places, pos, rows, out):
    size = out.shape[0] - (16 if with_places else 0)
    count = rows.shape[0]
    onehot = onehot_to(pos[...], base, size)
    out[:size] = jnp.dot(onehot, rows[...], preferred_element_type=jnp.float32).astype(out.dtype)
    if with_places:
        out[size:] = jnp.zeros((16, out.shape[1]), out.dtype)

        @pl.when(pl.program_id(0) == 0)
        def _():
            lines = jnp.concatenate(
                [pos[:, i * 128 : (i + 1) * 128] for i in range(count // 128)] + [jnp.zeros((8 - count // 128, 128), jnp.int32)],
                axis=0,
            )
            both = jnp.concatenate([lines // 256, lines % 256], axis=0)
            out[size:, :128] = both.astype(jnp.float32).astype(out.dtype)


def pack(h, pos, base, size, with_places):
    width = h.shape[1]
    part = width // COLUMN_PARTS
    count = pos.shape[1]
    out_rows = size + (16 if with_places else 0)
    return pl.pallas_call(
        functools.partial(pack_kernel, base, with_places),
        grid=(COLUMN_PARTS,),
        in_specs=[pl.BlockSpec((1, count), lambda j: (0, 0)), pl.BlockSpec((count, part), lambda j: (0, j))],
        out_specs=pl.BlockSpec((out_rows, part), lambda j: (0, j)),
        out_shape=jax.ShapeDtypeStruct((out_rows, width), h.dtype),
        compiler_params=PARAMS,
        cost_estimate=SMALL_COST,
        name="pack_rows",
    )(pos, h)


def merge_kernel(slots, rows, changed, out, onehot):
    size = rows.shape[0]

    @pl.when(pl.program_id(1) == 0)
    def _():
        line = lax.broadcasted_iota(jnp.int32, (size, size), 0)
        lane = lax.broadcasted_iota(jnp.int32, (size, size), 1)
        own = jnp.where((line == lane) & (slots[...] < 0), 1.0, 0.0)
        other = jnp.where(line == slots[...], 1.0, 0.0)
        onehot[...] = jnp.concatenate([own, other], axis=0).T.astype(jnp.bfloat16)

    both = jnp.concatenate([rows[...], changed[...]], axis=0)
    out[...] = jnp.dot(onehot[...], both, preferred_element_type=jnp.float32).astype(out.dtype)


def merge(h, slots, changed, first, tiles):
    size, width = changed.shape
    part = width // COLUMN_PARTS
    return pl.pallas_call(
        merge_kernel,
        grid=(tiles, COLUMN_PARTS),
        in_specs=[
            pl.BlockSpec((1, size), lambda i, j: (0, i + first)),
            pl.BlockSpec((size, part), lambda i, j: (i + first, j)),
            pl.BlockSpec((size, part), lambda i, j: (0, j)),
        ],
        out_specs=pl.BlockSpec((size, part), lambda i, j: (i, j)),
        out_shape=jax.ShapeDtypeStruct((tiles * size, width), h.dtype),
        scratch_shapes=[pltpu.VMEM((size, 2 * size), jnp.bfloat16)],
        compiler_params=PARAMS,
        cost_estimate=SMALL_COST,
        name="merge_rows",
    )(slots, h, changed)


def unpack_kernel(pos, early, late, out, onehot):
    @pl.when(pl.program_id(0) == 0)
    def _():
        onehot[...] = onehot_to(pos[...], 0, pos.shape[1]).astype(jnp.float32).T.astype(jnp.bfloat16)

    both = jnp.concatenate([early[...], late[...]], axis=0)
    out[...] = jnp.dot(onehot[...], both, preferred_element_type=jnp.float32).astype(out.dtype)


def unpack(pos, early, late, rows):
    size, width = late.shape
    part = width // COLUMN_PARTS
    count = pos.shape[1]
    return pl.pallas_call(
        unpack_kernel,
        grid=(COLUMN_PARTS,),
        in_specs=[
            pl.BlockSpec((1, count), lambda j: (0, 0)),
            pl.BlockSpec((count - size, part), lambda j: (0, j)),
            pl.BlockSpec((size, part), lambda j: (0, j)),
        ],
        out_specs=pl.BlockSpec((count, part), lambda j: (0, j)),
        out_shape=jax.ShapeDtypeStruct((rows, width), late.dtype),
        scratch_shapes=[pltpu.VMEM((count, count), jnp.bfloat16)],
        compiler_params=PARAMS,
        cost_estimate=SMALL_COST,
        name="unpack_rows",
    )(pos, early, late)


def put_kernel(piece, _, out):
    out[...] = piece[...]


def put(out, piece, first_row):
    step = 64
    width = piece.shape[1]
    return pl.pallas_call(
        put_kernel,
        grid=(piece.shape[0] // step,),
        in_specs=[pl.BlockSpec((step, width), lambda i: (i, 0)), pl.BlockSpec(memory_space=pl.ANY)],
        out_specs=pl.BlockSpec((step, width), lambda i: (i + first_row // step, 0)),
        out_shape=jax.ShapeDtypeStruct(out.shape, out.dtype),
        input_output_aliases={1: 0},
        compiler_params=PARAMS,
        cost_estimate=SMALL_COST,
        name="put_rows",
    )(piece, out)


def pack_last_kernel(base, pos, rows, out, total):
    step = pl.program_id(0)
    part = jnp.dot(onehot_to(pos[...], base, out.shape[0]), rows[...], preferred_element_type=jnp.float32)

    @pl.when(step == 0)
    def _():
        total[...] = part

    @pl.when(step > 0)
    def _():
        total[...] += part

    @pl.when(step == pl.num_programs(0) - 1)
    def _():
        out[...] = total[...].astype(out.dtype)


def pack_last(h, pos, base, size):
    rows, width = h.shape
    step = 2 * size
    return pl.pallas_call(
        functools.partial(pack_last_kernel, base),
        grid=(rows // step,),
        in_specs=[
            pl.BlockSpec((1, step), lambda i: (0, i)),
            pl.BlockSpec((step, width), lambda i: (i, 0)),
        ],
        out_specs=pl.BlockSpec((size, width), lambda i: (0, 0)),
        out_shape=jax.ShapeDtypeStruct((size, width), h.dtype),
        scratch_shapes=[pltpu.VMEM((size, width), jnp.float32)],
        compiler_params=pltpu.CompilerParams(vmem_limit_bytes=VMEM_LIMIT),
        cost_estimate=SMALL_COST,
        name="pack_last",
    )(pos, h)


def expert_rows(rows, gate_dev, up_dev, down_dev, out):
    gate = jnp.dot(rows[...], gate_dev[0], preferred_element_type=jnp.float32)
    upper = jnp.dot(rows[...], up_dev[0], preferred_element_type=jnp.float32)
    active = (jax.nn.silu(gate) * upper).astype(jnp.bfloat16)
    part = out.shape[1] // COLUMN_PARTS
    for j in range(COLUMN_PARTS):
        columns = slice(j * part, (j + 1) * part)
        out[:, columns] = jnp.dot(
            active, down_dev[0, :, columns], preferred_element_type=jnp.float32
        ).astype(out.dtype)


def update_kernel(
    last, picked, beside, keep, gain, router, gate_dev, up_dev, down_dev, out, out_beside,
    normed, normed_got, own_part, sent_part, got_part, sems,
):
    other = 1 - lax.axis_index("expert")
    barrier = pltpu.get_barrier_semaphore()
    pl.semaphore_signal(barrier, inc=1, device_id={"expert": other}, device_id_type=pl.DeviceIdType.MESH)

    last32 = last[...].astype(jnp.float32)
    var = jnp.mean(last32 * last32, axis=-1, keepdims=True)
    normed[...] = (last32 * lax.rsqrt(var + 1e-06) * gain[...]).astype(normed.dtype)
    pl.semaphore_wait(barrier, 1)
    rows_copy = pltpu.make_async_remote_copy(
        src_ref=normed, dst_ref=normed_got, send_sem=sems.at[0], recv_sem=sems.at[1],
        device_id={"expert": other}, device_id_type=pl.DeviceIdType.MESH,
    )
    rows_copy.start()

    scores = jax.nn.sigmoid(jnp.dot(normed[...], router[0], preferred_element_type=jnp.float32))
    named = scores * picked[...]
    weight = 2.5 * named[:, 0:1] / jnp.sum(named, axis=-1, keepdims=True)
    expert_rows(normed, gate_dev, up_dev, down_dev, own_part)

    rows_copy.wait()
    expert_rows(normed_got, gate_dev, up_dev, down_dev, sent_part)
    part_copy = pltpu.make_async_remote_copy(
        src_ref=sent_part, dst_ref=got_part, send_sem=sems.at[2], recv_sem=sems.at[3],
        device_id={"expert": other}, device_id_type=pl.DeviceIdType.MESH,
    )
    part_copy.start()
    part_copy.wait()
    summed = own_part[...].astype(jnp.float32) + got_part[...].astype(jnp.float32)
    out[...] = (last[...].astype(jnp.float32) + summed * weight).astype(out.dtype)
    out_beside[...] = jnp.where(keep[...] > 0.0, out[...].astype(jnp.float32), beside[...].astype(jnp.float32)).astype(out.dtype)


def update(last, picked, beside, keep, norm_gain, router, w_gate, w_up, w_down):
    block = pltpu.VMEM(last.shape, last.dtype)
    return pl.pallas_call(
        update_kernel,
        in_specs=[pl.BlockSpec(memory_space=pltpu.VMEM)] * 9,
        out_specs=[pl.BlockSpec(memory_space=pltpu.VMEM)] * 2,
        out_shape=[jax.ShapeDtypeStruct(last.shape, last.dtype)] * 2,
        scratch_shapes=[block] * 5 + [pltpu.SemaphoreType.DMA((4,))],
        compiler_params=pltpu.CompilerParams(
            collective_id=0, has_side_effects=True, vmem_limit_bytes=VMEM_LIMIT
        ),
        cost_estimate=SMALL_COST,
        name="expert_update",
    )(last, picked, beside, keep, norm_gain, router, w_gate, w_up, w_down)


def local(state, norm_gain, router, w_gate, w_up, w_down, route_ids):
    h = state[0]
    rows = h.shape[0]
    size = rows // 8
    early_rows = EARLY * size
    head_rows = early_rows + size
    ids = route_ids[0, 0]

    chosen = jnp.sum((ids == 0).astype(jnp.int32), axis=-1)
    slot = (jnp.cumsum(chosen) - chosen).astype(jnp.int32)
    kept = (chosen > 0) & (slot < size)
    slots = jnp.where(kept, slot, -1)[None, :]
    count = jnp.minimum(jnp.sum(chosen[:head_rows]), size)
    other = jnp.arange(rows, dtype=jnp.int32) - jnp.minimum(slot, size)
    pos = jnp.where(kept, early_rows + slot, jnp.where(other < early_rows, other, other + count))
    pos = pos[None, :head_rows].astype(jnp.int32)

    early = pack(h, pos, 0, early_rows, True)
    moved_early = passed_along(early, "section", 1)
    slots = after(slots, early)
    last = pack_last(h, slots, 0, size)
    beside = pack(h, after(pos, early), early_rows, size, False)

    last_ids = jnp.dot(
        onehot_to(slots, 0, size), ids.astype(jnp.bfloat16), preferred_element_type=jnp.float32
    )
    experts = jnp.arange(router.shape[2]).astype(jnp.float32)
    picked = jnp.sum((last_ids[:, :, None] == experts[None, None, :]).astype(jnp.float32), axis=1)
    keep = (jnp.arange(size) < count).astype(jnp.float32)[:, None]
    changed, beside = update(last, picked, beside, keep, norm_gain, router, w_gate, w_up, w_down)
    moved_beside = passed_along(beside, "section", 1)

    first = EARLY + 1
    second = merge(h, slots, changed, first, 2)
    third = merge(h, slots, after(changed, second), first + 2, 1)
    fourth = merge(h, slots, after(changed, third), first + 3, 1)
    moved_second = passed_along(second, "section", 1)
    moved_third = passed_along(after(third, moved_early), "section", 1)
    moved_fourth = passed_along(after(fourth, moved_second), "section", 1)

    places = moved_early[early_rows:, :128].astype(jnp.int32)
    lines = head_rows // 128
    moved_pos = (places[:lines] * 256 + places[8 : 8 + lines]).reshape(1, head_rows)
    out = unpack(moved_pos, moved_early, moved_beside, rows)
    out = put(out, moved_second, first * size)
    out = put(out, moved_third, (first + 2) * size)
    out = put(out, moved_fourth, (first + 3) * size)
    return out[None]


def solution(mesh):
    return jax.shard_map(
        local,
        mesh=mesh,
        in_specs=(
            P("section", "expert", None),
            P("section", None),
            P("section", None, None),
            P("section", None, "expert"),
            P("section", None, "expert"),
            P("section", "expert", None),
            P(None, "section", "expert", None),
        ),
        out_specs=P("section", "expert", None),
        check_vma=False,
    )
```

time: 198 us -> 180 us (0.909)
  waiting for transfers between devices: 120 us -> 105 us
  Pallas kernels: 62.4 us -> 58.7 us
    ppermute x4 -> x5, waiting for transfers between devices: 120 us -> 105 us  [passed_along(): lax.ppermute(x, axis, [(i, (i + by) % devices) for i in range(devices)])]
    pallas_call x5 -> x9, Pallas kernels: 43 us -> 38.9 us  [the longest x3 15.5 us: merge(): pl.pallas_call(merge_kernel, grid=(tiles, COLUMN_PARTS), in_specs=[pl.Blo...]
    ppermute x4 -> x5, starting transfers between devices: 6.04 us -> 6.42 us  [passed_along(): lax.ppermute(x, axis, [(i, (i + by) % devices) for i in range(devices)])]
  transfers between devices with their start and end apart: 4 -> 5, of which waited for: 3 -> 4; matrix products, arithmetic and copies ran while one was open for 1% -> 2% of each run, Pallas kernels for 19% -> 29%
where the time goes in v3:
time: 180 us; the launch traced here: 179 us
  waiting for transfers between devices  105 us (58%)
  Pallas kernels  58.7 us (33%)
  starting transfers between devices  6.42 us (4%)
  other arithmetic  4.82 us (3%)
  local copies, waits for them, and re-layouts  2.68 us (1%)
    ppermute x5, waiting for transfers between devices, passed_along(): lax.ppermute(x, axis, [(i, (i + by) % devices) for i in range(devices)])  105 us
    pallas_call x3, Pallas kernels, merge(): pl.pallas_call(merge_kernel, grid=(tiles, COLUMN_PARTS), in_specs=[pl.Blo...  15.5 us
    pallas_call x1, Pallas kernels, update(): pl.pallas_call(update_kernel, in_specs=[pl.BlockSpec(memory_space=pltpu.V...  13.9 us
    pallas_call x2, Pallas kernels, pack(): pl.pallas_call(functools.partial(pack_kernel, base, with_places), grid=(C...  9.75 us
    pallas_call x3, Pallas kernels, put(): pl.pallas_call(put_kernel, grid=(piece.shape[0] // step,), in_specs=[pl.B...  7.61 us
    ppermute x5, starting transfers between devices, passed_along(): lax.ppermute(x, axis, [(i, (i + by) % devices) for i in range(devices)])  6.42 us
    pallas_call x1, Pallas kernels, unpack(): pl.pallas_call(unpack_kernel, grid=(COLUMN_PARTS,), in_specs=[pl.BlockSpe...  6 us
    pallas_call x1, Pallas kernels, pack_last(): pl.pallas_call(functools.partial(pack_last_kernel, base), grid=(rows // s...  5.95 us
  transfers between devices with their start and end apart: 5, of which 4 were waited for; matrix products, arithmetic and copies ran while one was open for 2% of the time, Pallas kernels for 29%

profile of v3, /device:TPU:0, one launch (start us, length us, event | category | flops | bytes accessed | tf_op | source)
XLA Modules:
  0.0 179.0 jit_solution(9230819112594853773)
XLA Ops:
  0.0 0.8 convert_reduce_fusion.1
  0.8 0.6 slice_reduce_fusion.1
  1.4 0.3 reduce-window.9
  1.7 0.1 slice.22
  1.8 0.1 slice_reduce_fusion
  2.6 0.1 fusion.7
  2.6 0.6 slice.25
  3.2 5.3 %pack_rows.2 = bf16[400,3584]{1,0:T(8,128)(2,1)} custom-call(s32[1,512]{1,0:T(1,128)} %bitcast.24, bf16[1024,3584]{1,0:T(8,128)(2,1)} %bitcast.15), custom_call_target="tpu_custom_call" | custom-call | flops 1024 | bytes 1024 | tf_op jit(solution)/shard_map/pack_rows/pallas_call | solution.py:54
  8.5 2.9 %collective-permute-start.2 = (bf16[400,3584]{1,0:T(8,128)(2,1)}, bf16[400,3584]{1,0:T(8,128)(2,1)S(1)}, u32[]{:S(2)}, u32[]{:S(2)}) collective-permute-start(bf16[400,3584]{1,0:T(8,128)(2,1)} %pack_rows.2), channel_id=1, source_target_pairs={{0,2},{2,4},{4,6},{6,8},{8,10},{10,12},{12,14},{14,16},{16,18},{18... | collective-permute-start | bytes 8601608 | tf_op jit(solution)/shard_map/ppermute | solution.py:19
  11.5 4.5 %pack_rows.3.beside = bf16[128,3584]{1,0:T(8,128)(2,1)} custom-call(s32[1,512]{1,0:T(1,128)} %bitcast.25, bf16[1024,3584]{1,0:T(8,128)(2,1)} %bitcast.16), custom_call_target="tpu_custom_call" | custom-call | flops 1024 | bytes 1024 | tf_op jit(solution)/shard_map/pack_rows/pallas_call | solution.py:54
  15.9 0.6 and_select_fusion.pos.slots
  16.5 0.0 copy-start.5
  16.5 0.0 copy-start.6
  16.5 6.0 %pack_last.1.last = bf16[128,3584]{1,0:T(8,128)(2,1)} custom-call(s32[1,1024]{1,0:T(1,128)} %and_select_fusion.pos.slots, bf16[1024,3584]{1,0:T(8,128)(2,1)} %bitcast.17), custom_call_target="tpu_custom_call" | custom-call | flops 1024 | bytes 1024 | tf_op jit(solution)/shard_map/pack_last/pallas_call | solution.py:171
  22.5 0.6 fusion.4.keep
  23.1 0.0 copy-done.5
  23.1 0.0 copy-done.6
  23.1 0.2 fusion
  23.3 0.8 convert_reduce_fusion.picked
  24.2 13.9 %expert_update.1 = (bf16[128,3584]{1,0:T(8,128)(2,1)}, bf16[128,3584]{1,0:T(8,128)(2,1)}) custom-call(bf16[128,3584]{1,0:T(8,128)(2,1)} %pack_last.1.last, f32[128,128]{1,0:T(8,128)} %convert_reduce_fusion.picked, bf16[128,3584]{1,0:T(8,128)(2,1)} %pack_rows.3.beside, f32[128,1]{1,0:T(8,128)} %fusion.4.keep, f32[1,3584]{1,0:T(1,128)} %gain.1, ...), custom_call_target="tpu_custom_call" | custom-call | flops 1024 | bytes 1024 | tf_op jit(solution)/shard_map/expert_update/pallas_call | solution.py:237
  38.1 7.1 %merge_rows.3 = bf16[256,3584]{1,0:T(8,128)(2,1)} custom-call(s32[1,1024]{1,0:T(1,128)} %and_select_fusion.pos.slots, bf16[1024,3584]{1,0:T(8,128)(2,1)} %bitcast.18, bf16[128,3584]{1,0:T(8,128)(2,1)} %get-tuple-element.17.changed), custom_call_target="tpu_custom_call" | custom-call | flops 1024 | bytes 1024 | tf_op jit(solution)/shard_map/merge_rows/pallas_call | solution.py:84
  45.2 1.5 collective-permute-start
  46.7 1.5 collective-permute-start.4
  48.2 4.1 %merge_rows.4 = bf16[128,3584]{1,0:T(8,128)(2,1)} custom-call(s32[1,1024]{1,0:T(1,128)} %and_select_fusion.pos.slots, bf16[1024,3584]{1,0:T(8,128)(2,1)} %bitcast.19, bf16[128,3584]{1,0:T(8,128)(2,1)} %get-tuple-element.17.changed), custom_call_target="tpu_custom_call" | custom-call | flops 1024 | bytes 1024 | tf_op jit(solution)/shard_map/merge_rows/pallas_call | solution.py:84
  52.4 0.0 copy-start.3
  52.4 4.2 %merge_rows.5 = bf16[128,3584]{1,0:T(8,128)(2,1)} custom-call(s32[1,1024]{1,0:T(1,128)} %and_select_fusion.pos.slots, bf16[1024,3584]{1,0:T(8,128)(2,1)} %bitcast.20, bf16[128,3584]{1,0:T(8,128)(2,1)} %get-tuple-element.17.changed), custom_call_target="tpu_custom_call" | custom-call | flops 1024 | bytes 1024 | tf_op jit(solution)/shard_map/merge_rows/pallas_call | solution.py:84
  56.6 61.3 %collective-permute-done.piece = bf16[256,3584]{1,0:T(8,128)(2,1)S(1)} collective-permute-done((bf16[256,3584]{1,0:T(8,128)(2,1)}, bf16[256,3584]{1,0:T(8,128)(2,1)S(1)}, u32[]{:S(2)}, u32[]{:S(2)}) %collective-permute-start) | collective-permute-done | bytes 1835040 | tf_op jit(solution)/shard_map/ppermute | solution.py:19
  117.9 0.0 copy-start.1
  117.9 0.0 collective-permute-done.2.early
  117.9 0.0 copy-done.3
  118.0 0.0 copy-start
  118.0 0.1 collective-permute-start.3
  118.0 0.4 collective-permute-start.1
  118.5 0.9 slice_add_fusion
  119.4 18.2 %collective-permute-done.4.late = bf16[128,3584]{1,0:T(8,128)(2,1)S(1)} collective-permute-done((bf16[128,3584]{1,0:T(8,128)(2,1)}, bf16[128,3584]{1,0:T(8,128)(2,1)S(1)}, u32[]{:S(2)}, u32[]{:S(2)}) %collective-permute-start.4) | collective-permute-done | bytes 917536 | tf_op jit(solution)/shard_map/ppermute | solution.py:19
  137.6 0.0 copy-start.2
  137.6 0.0 copy-done
  137.6 0.9 copy-done.2
  138.6 6.0 %unpack_rows.1._ = bf16[1024,3584]{1,0:T(8,128)(2,1)} custom-call(s32[1,512]{1,0:T(1,128)} %bitcast.27, bf16[400,3584]{1,0:T(8,128)(2,1)} %copy-done, bf16[128,3584]{1,0:T(8,128)(2,1)} %copy-done.2), custom_call_target="tpu_custom_call" | custom-call | flops 1024 | bytes 1024 | tf_op jit(solution)/shard_map/unpack_rows/pallas_call | solution.py:114
  144.6 0.0 copy-done.1
  144.6 3.7 %put_rows.3._ = bf16[1024,3584]{1,0:T(8,128)(2,1)} custom-call(bf16[256,3584]{1,0:T(8,128)(2,1)} %copy-done.1, bf16[1024,3584]{1,0:T(8,128)(2,1)} %unpack_rows.1._), custom_call_target="tpu_custom_call", output_to_operand_aliasing={{}: (1, {})} | custom-call | flops 1024 | bytes 1024 | tf_op jit(solution)/shard_map/put_rows/pallas_call | solution.py:138
  148.2 9.1 %collective-permute-done.3.piece = bf16[128,3584]{1,0:T(8,128)(2,1)} collective-permute-done((bf16[128,3584]{1,0:T(8,128)(2,1)S(1)}, bf16[128,3584]{1,0:T(8,128)(2,1)}, u32[]{:S(2)}, u32[]{:S(2)}) %collective-permute-start.3) | collective-permute-done | bytes 917536 | tf_op jit(solution)/shard_map/ppermute | solution.py:19
  157.4 2.0 %put_rows.4._ = bf16[1024,3584]{1,0:T(8,128)(2,1)} custom-call(bf16[128,3584]{1,0:T(8,128)(2,1)} %collective-permute-done.3.piece, bf16[1024,3584]{1,0:T(8,128)(2,1)} %put_rows.3._), custom_call_target="tpu_custom_call", output_to_operand_aliasing={{}: (1, {})} | custom-call | flops 1024 | bytes 1024 | tf_op jit(solution)/shard_map/put_rows/pallas_call | solution.py:138
  159.3 16.8 %collective-permute-done.1.piece = bf16[128,3584]{1,0:T(8,128)(2,1)S(1)} collective-permute-done((bf16[128,3584]{1,0:T(8,128)(2,1)}, bf16[128,3584]{1,0:T(8,128)(2,1)S(1)}, u32[]{:S(2)}, u32[]{:S(2)}) %collective-permute-start.1) | collective-permute-done | bytes 917536 | tf_op jit(solution)/shard_map/ppermute | solution.py:19
  176.1 0.0 copy-start.4
  176.1 0.9 copy-done.4
  177.0 2.0 %put_rows.5 = bf16[1024,3584]{1,0:T(8,128)(2,1)} custom-call(bf16[128,3584]{1,0:T(8,128)(2,1)} %copy-done.4, bf16[1024,3584]{1,0:T(8,128)(2,1)} %put_rows.4._), custom_call_target="tpu_custom_call", output_to_operand_aliasing={{}: (1, {})} | custom-call | flops 1024 | bytes 1024 | tf_op jit(solution)/shard_map/put_rows/pallas_call | solution.py:138
  (3 shorter events, 0.0 us)
Async XLA Ops:
  8.5 109.4 %collective-permute-start.2 = (bf16[400,3584]{1,0:T(8,128)(2,1)}, bf16[400,3584]{1,0:T(8,128)(2,1)S(1)}, u32[]{:S(2)}, u32[]{:S(2)}) collective-permute-start(bf16[400,3584]{1,0:T(8,128)(2,1)} %pack_rows.2), channel_id=1, source_target_pairs={{0,2},{2,4},{4,6},{6,8},{8,10},{10,12},{12,14},{14,16},{16,18},{18... | collective-permute-start | bytes 8601608 | tf_op jit(solution)/shard_map/ppermute | solution.py:19
  16.5 6.6 %copy-start.5 = (s32[1,1024]{1,0:T(1,128)S(1)}, s32[1,1024]{1,0:T(1,128)}, u32[]{:S(2)}) copy-start(s32[1,1024]{1,0:T(1,128)} %and_select_fusion.pos.slots) | copy-start | bytes 12292
  16.5 6.6 %copy-start.6 = (s32[1,1,1024,8]{2,3,1,0:T(8,128)S(1)}, s32[1,1,1024,8]{2,3,1,0:T(8,128)}, u32[]{:S(2)}) copy-start(s32[1,1,1024,8]{2,3,1,0:T(8,128)} %param.13) | copy-start | bytes 98308
  45.2 72.7 %collective-permute-start = (bf16[256,3584]{1,0:T(8,128)(2,1)}, bf16[256,3584]{1,0:T(8,128)(2,1)S(1)}, u32[]{:S(2)}, u32[]{:S(2)}) collective-permute-start(bf16[256,3584]{1,0:T(8,128)(2,1)} %merge_rows.3), channel_id=1, source_target_pairs={{0,2},{2,4},{4,6},{6,8},{8,10},{10,12},{12,14},{14,16},{16,18},{18... | collective-permute-start | bytes 5505032 | tf_op jit(solution)/shard_map/ppermute | solution.py:19
  46.7 90.9 %collective-permute-start.4 = (bf16[128,3584]{1,0:T(8,128)(2,1)}, bf16[128,3584]{1,0:T(8,128)(2,1)S(1)}, u32[]{:S(2)}, u32[]{:S(2)}) collective-permute-start(bf16[128,3584]{1,0:T(8,128)(2,1)} %get-tuple-element.20), channel_id=1, source_target_pairs={{0,2},{2,4},{4,6},{6,8},{8,10},{10,12},{12,14},{14,16},{16,18},{18... | collective-permute-start | bytes 2752520 | tf_op jit(solution)/shard_map/ppermute | solution.py:19
  52.4 65.6 %copy-start.3 = (bf16[128,3584]{1,0:T(8,128)(2,1)S(1)}, bf16[128,3584]{1,0:T(8,128)(2,1)}, u32[]{:S(2)}) copy-start(bf16[128,3584]{1,0:T(8,128)(2,1)} %merge_rows.4) | copy-start | bytes 2752516
  117.9 26.6 %copy-start.1 = (bf16[256,3584]{1,0:T(8,128)(2,1)}, bf16[256,3584]{1,0:T(8,128)(2,1)S(1)}, u32[]{:S(2)}) copy-start(bf16[256,3584]{1,0:T(8,128)(2,1)S(1)} %collective-permute-done.piece) | copy-start | bytes 5505028
  118.0 19.7 %copy-start = (bf16[400,3584]{1,0:T(8,128)(2,1)}, bf16[400,3584]{1,0:T(8,128)(2,1)S(1)}, u32[]{:S(2)}) copy-start(bf16[400,3584]{1,0:T(8,128)(2,1)S(1)} %collective-permute-done.2.early) | copy-start | bytes 8601604
  118.0 39.4 %collective-permute-start.3 = (bf16[128,3584]{1,0:T(8,128)(2,1)S(1)}, bf16[128,3584]{1,0:T(8,128)(2,1)}, u32[]{:S(2)}, u32[]{:S(2)}) collective-permute-start(bf16[128,3584]{1,0:T(8,128)(2,1)S(1)} %copy-done.3), channel_id=1, source_target_pairs={{0,2},{2,4},{4,6},{6,8},{8,10},{10,12},{12,14},{14,16},{16,18},{18... | collective-permute-start | bytes 2752520 | tf_op jit(solution)/shard_map/ppermute | solution.py:19
  118.0 58.1 %collective-permute-start.1 = (bf16[128,3584]{1,0:T(8,128)(2,1)}, bf16[128,3584]{1,0:T(8,128)(2,1)S(1)}, u32[]{:S(2)}, u32[]{:S(2)}) collective-permute-start(bf16[128,3584]{1,0:T(8,128)(2,1)} %merge_rows.5), channel_id=1, source_target_pairs={{0,2},{2,4},{4,6},{6,8},{8,10},{10,12},{12,14},{14,16},{16,18},{18... | collective-permute-start | bytes 2752520 | tf_op jit(solution)/shard_map/ppermute | solution.py:19
  137.6 0.9 copy-start.2
  176.1 0.9 copy-start.4

commit v4 on v3

--- a/solution.py
+++ b/solution.py
@@ -9,7 +9,7 @@
 
 VMEM_LIMIT = 56 * 1024 * 1024
 COLUMN_PARTS = 4
-EARLY = 3
+EARLY = 2
 SMALL_COST = pl.CostEstimate(flops=1024, bytes_accessed=1024, transcendentals=0)
 PARAMS = pltpu.CompilerParams(vmem_limit_bytes=VMEM_LIMIT)
 
@@ -28,35 +28,72 @@
     return jnp.where(places == pos, 1.0, 0.0).astype(jnp.bfloat16)
 
 
-def pack_kernel(base, with_places, pos, rows, out):
-    size = out.shape[0] - (16 if with_places else 0)
+def pack_early_kernel(cap, chosen, rows, out, pos):
+    size = out.shape[0] - 16
     count = rows.shape[0]
-    onehot = onehot_to(pos[...], base, size)
+
+    @pl.when(pl.program_id(0) == 0)
+    def _():
+        line = lax.broadcasted_iota(jnp.int32, (count, count), 0)
+        lane = lax.broadcasted_iota(jnp.int32, (count, count), 1)
+        ahead = jnp.where(line < lane, 1.0, 0.0).astype(jnp.bfloat16)
+        named = chosen[...]
+        flags = jnp.broadcast_to(named, (16, count)).astype(jnp.bfloat16)
+        slot = jnp.dot(flags, ahead, preferred_element_type=jnp.float32)[0:1].astype(jnp.int32)
+        total = jnp.minimum(jnp.sum(named, axis=1, keepdims=True).astype(jnp.int32), cap)
+        other = lane[0:1] - jnp.minimum(slot, cap)
+        late = jnp.where(other < size, other, other + total)
+        places = jnp.where((named > 0.0) & (slot < cap), size + slot, late)
+        pos[...] = places
+        lines = jnp.concatenate(
+            [places[:, i * 128 : (i + 1) * 128] for i in range(count // 128)]
+            + [jnp.zeros((8 - count // 128, 128), jnp.int32)],
+            axis=0,
+        )
+        both = jnp.concatenate([lines // 256, lines % 256], axis=0)
+        out[size:, :128] = both.astype(jnp.float32).astype(out.dtype)
+        out[size:, 128:] = jnp.zeros((16, out.shape[1] - 128), out.dtype)
+
+    @pl.when(pl.program_id(0) > 0)
+    def _():
+        out[size:] = jnp.zeros((16, out.shape[1]), out.dtype)
+
+    onehot = onehot_to(pos[...], 0, size)
     out[:size] = jnp.dot(onehot, rows[...], preferred_element_type=jnp.float32).astype(out.dtype)
-    if with_places:
-        out[size:] = jnp.zeros((16, out.shape[1]), out.dtype)
-
-        @pl.when(pl.program_id(0) == 0)
-        def _():
-            lines = jnp.concatenate(
-                [pos[:, i * 128 : (i + 1) * 128] for i in range(count // 128)] + [jnp.zeros((8 - count // 128, 128), jnp.int32)],
-                axis=0,
-            )
-            both = jnp.concatenate([lines // 256, lines % 256], axis=0)
-            out[size:, :128] = both.astype(jnp.float32).astype(out.dtype)
-
-
-def pack(h, pos, base, size, with_places):
+
+
+def pack_early(h, chosen, size, cap):
+    width = h.shape[1]
+    part = width // COLUMN_PARTS
+    count = size + cap
+    return pl.pallas_call(
+        functools.partial(pack_early_kernel, cap),
+        grid=(COLUMN_PARTS,),
+        in_specs=[pl.BlockSpec((1, count), lambda j: (0, 0)), pl.BlockSpec((count, part), lambda j: (0, j))],
+        out_specs=pl.BlockSpec((size + 16, part), lambda j: (0, j)),
+        out_shape=jax.ShapeDtypeStruct((size + 16, width), h.dtype),
+        scratch_shapes=[pltpu.VMEM((1, count), jnp.int32)],
+        compiler_params=PARAMS,
+        cost_estimate=SMALL_COST,
+        name="pack_early",
+    )(chosen, h)
+
+
+def pack_kernel(base, pos, rows, out):
+    onehot = onehot_to(pos[...], base, out.shape[0])
+    out[...] = jnp.dot(onehot, rows[...], preferred_element_type=jnp.float32).astype(out.dtype)
+
+
+def pack(h, pos, base, size):
     width = h.shape[1]
     part = width // COLUMN_PARTS
     count = pos.shape[1]
-    out_rows = size + (16 if with_places else 0)
-    return pl.pallas_call(
-        functools.partial(pack_kernel, base, with_places),
+    return pl.pallas_call(
+        functools.partial(pack_kernel, base),
         grid=(COLUMN_PARTS,),
         in_specs=[pl.BlockSpec((1, count), lambda j: (0, 0)), pl.BlockSpec((count, part), lambda j: (0, j))],
-        out_specs=pl.BlockSpec((out_rows, part), lambda j: (0, j)),
-        out_shape=jax.ShapeDtypeStruct((out_rows, width), h.dtype),
+        out_specs=pl.BlockSpec((size, part), lambda j: (0, j)),
+        out_shape=jax.ShapeDtypeStruct((size, width), h.dtype),
         compiler_params=PARAMS,
         cost_estimate=SMALL_COST,
         name="pack_rows",
@@ -128,21 +165,21 @@
     )(pos, early, late)
 
 
-def put_kernel(piece, _, out):
-    out[...] = piece[...]
+def put_kernel(first_row, piece, _, out, sem):
+    copy = pltpu.make_async_copy(piece, out.at[pl.ds(first_row, piece.shape[0])], sem)
+    copy.start()
+    copy.wait()
 
 
 def put(out, piece, first_row):
-    step = 64
-    width = piece.shape[1]
-    return pl.pallas_call(
-        put_kernel,
-        grid=(piece.shape[0] // step,),
-        in_specs=[pl.BlockSpec((step, width), lambda i: (i, 0)), pl.BlockSpec(memory_space=pl.ANY)],
-        out_specs=pl.BlockSpec((step, width), lambda i: (i + first_row // step, 0)),
+    return pl.pallas_call(
+        functools.partial(put_kernel, first_row),
+        in_specs=[pl.BlockSpec(memory_space=pl.ANY)] * 2,
+        out_specs=pl.BlockSpec(memory_space=pl.ANY),
         out_shape=jax.ShapeDtypeStruct(out.shape, out.dtype),
+        scratch_shapes=[pltpu.SemaphoreType.DMA],
         input_output_aliases={1: 0},
-        compiler_params=PARAMS,
+        compiler_params=pltpu.CompilerParams(vmem_limit_bytes=1024 * 1024),
         cost_estimate=SMALL_COST,
         name="put_rows",
     )(piece, out)
@@ -265,11 +302,11 @@
     pos = jnp.where(kept, early_rows + slot, jnp.where(other < early_rows, other, other + count))
     pos = pos[None, :head_rows].astype(jnp.int32)
 
-    early = pack(h, pos, 0, early_rows, True)
+    early = pack_early(h, chosen.astype(jnp.float32)[None, :], early_rows, size)
     moved_early = passed_along(early, "section", 1)
     slots = after(slots, early)
     last = pack_last(h, slots, 0, size)
-    beside = pack(h, after(pos, early), early_rows, size, False)
+    beside = pack(h, after(pos, early), early_rows, size)
 
     last_ids = jnp.dot(
         onehot_to(slots, 0, size), ids.astype(jnp.bfloat16), preferred_element_type=jnp.float32
@@ -282,8 +319,8 @@
 
     first = EARLY + 1
     second = merge(h, slots, changed, first, 2)
-    third = merge(h, slots, after(changed, second), first + 2, 1)
-    fourth = merge(h, slots, after(changed, third), first + 3, 1)
+    third = merge(h, slots, after(changed, second), first + 2, 2)
+    fourth = merge(h, slots, after(changed, third), first + 4, 1)
     moved_second = passed_along(second, "section", 1)
     moved_third = passed_along(after(third, moved_early), "section", 1)
     moved_fourth = passed_along(after(fourth, moved_second), "section", 1)
@@ -294,7 +331,7 @@
     out = unpack(moved_pos, moved_early, moved_beside, rows)
     out = put(out, moved_second, first * size)
     out = put(out, moved_third, (first + 2) * size)
-    out = put(out, moved_fourth, (first + 3) * size)
+    out = put(out, moved_fourth, (first + 4) * size)
     return out[None]
 
 

time: 180 us -> 175 us (0.972)
  Pallas kernels: 58.7 us -> 56.1 us
    pallas_call x5, Pallas kernels: 17.4 us -> 12.5 us  [the longest x1 4.8 us: pack_early(): pl.pallas_call(functools.partial(pack_early_kernel, cap), grid=(COLUMN_PA...]
    pallas_call x3, Pallas kernels: 15.5 us -> 18.6 us  [merge(): pl.pallas_call(merge_kernel, grid=(tiles, COLUMN_PARTS), in_specs=[pl.Blo...]
  transfers between devices with their start and end apart: 5 -> 5, of which waited for: 4 -> 4; matrix products, arithmetic and copies ran while one was open for 2% -> 3% of each run, Pallas kernels for 29% -> 29%
where the time goes in v4:
time: 175 us
  waiting for transfers between devices  106 us (61%)
  Pallas kernels  56.1 us (32%)
  starting transfers between devices  4.94 us (3%)
  other arithmetic  4.55 us (3%)
  local copies, waits for them, and re-layouts  2.27 us (1%)
    ppermute x5, waiting for transfers between devices, passed_along(): lax.ppermute(x, axis, [(i, (i + by) % devices) for i in range(devices)])  106 us
    pallas_call x3, Pallas kernels, merge(): pl.pallas_call(merge_kernel, grid=(tiles, COLUMN_PARTS), in_specs=[pl.Blo...  18.6 us
    pallas_call x1, Pallas kernels, update(): pl.pallas_call(update_kernel, in_specs=[pl.BlockSpec(memory_space=pltpu.V...  13.9 us
    pallas_call x1, Pallas kernels, pack_last(): pl.pallas_call(functools.partial(pack_last_kernel, base), grid=(rows // s...  5.95 us
    pallas_call x1, Pallas kernels, unpack(): pl.pallas_call(unpack_kernel, grid=(COLUMN_PARTS,), in_specs=[pl.BlockSpe...  5.16 us
    ppermute x5, starting transfers between devices, passed_along(): lax.ppermute(x, axis, [(i, (i + by) % devices) for i in range(devices)])  4.94 us
    pallas_call x1, Pallas kernels, pack_early(): pl.pallas_call(functools.partial(pack_early_kernel, cap), grid=(COLUMN_PA...  4.8 us
    pallas_call x1, Pallas kernels, pack(): pl.pallas_call(functools.partial(pack_kernel, base), grid=(COLUMN_PARTS,)...  4.26 us
  transfers between devices with their start and end apart: 5, of which 4 were waited for; matrix products, arithmetic and copies ran while one was open for 3% of the time, Pallas kernels for 29%

profile of v4, /device:TPU:0, one launch (start us, length us, event | category | flops | bytes accessed | tf_op | source)
XLA Modules:
  0.0 174.7 jit_solution(13103322286925790697)
XLA Ops:
  0.0 0.8 convert_reduce_fusion.1
  0.8 0.6 convert_element_type.47.chosen
  1.4 4.8 %pack_early.1 = bf16[272,3584]{1,0:T(8,128)(2,1)} custom-call(f32[1,1024]{1,0:T(1,128)} %convert_element_type.47.chosen, bf16[1024,3584]{1,0:T(8,128)(2,1)} %bitcast.19), custom_call_target="tpu_custom_call" | custom-call | flops 1024 | bytes 1024 | tf_op jit(solution)/shard_map/pack_early/pallas_call | solution.py:69
  6.2 2.9 %collective-permute-start.2 = (bf16[272,3584]{1,0:T(8,128)(2,1)}, bf16[272,3584]{1,0:T(8,128)(2,1)S(1)}, u32[]{:S(2)}, u32[]{:S(2)}) collective-permute-start(bf16[272,3584]{1,0:T(8,128)(2,1)} %pack_early.1), channel_id=1, source_target_pairs={{0,2},{2,4},{4,6},{6,8},{8,10},{10,12},{12,14},{14,16},{16,18},{18... | collective-permute-start | bytes 5849096 | tf_op jit(solution)/shard_map/ppermute | solution.py:19
  9.1 0.7 slice_reduce_fusion.1
  9.8 0.3 reduce-window.9
  10.1 0.1 slice.22
  10.2 0.1 slice_reduce_fusion
  11.0 0.1 fusion.7
  11.1 0.5 broadcast_in_dim.26.pos
  11.6 4.3 %pack_rows.1.beside = bf16[128,3584]{1,0:T(8,128)(2,1)} custom-call(s32[1,384]{1,0:T(1,128)} %broadcast_in_dim.26.pos, bf16[1024,3584]{1,0:T(8,128)(2,1)} %bitcast.20), custom_call_target="tpu_custom_call" | custom-call | flops 1024 | bytes 1024 | tf_op jit(solution)/shard_map/pack_rows/pallas_call | solution.py:91
  15.9 0.6 and_select_fusion.pos.slots
  16.5 0.0 copy-start.2
  16.5 0.0 copy-start.3
  16.5 5.9 %pack_last.1.last = bf16[128,3584]{1,0:T(8,128)(2,1)} custom-call(s32[1,1024]{1,0:T(1,128)} %and_select_fusion.pos.slots, bf16[1024,3584]{1,0:T(8,128)(2,1)} %bitcast.21), custom_call_target="tpu_custom_call" | custom-call | flops 1024 | bytes 1024 | tf_op jit(solution)/shard_map/pack_last/pallas_call | solution.py:208
  22.5 0.6 fusion.4.keep
  23.1 0.0 copy-done.2
  23.1 0.0 copy-done.3
  23.1 0.2 fusion
  23.3 0.8 convert_reduce_fusion.picked
  24.2 13.9 %expert_update.1 = (bf16[128,3584]{1,0:T(8,128)(2,1)}, bf16[128,3584]{1,0:T(8,128)(2,1)}) custom-call(bf16[128,3584]{1,0:T(8,128)(2,1)} %pack_last.1.last, f32[128,128]{1,0:T(8,128)} %convert_reduce_fusion.picked, bf16[128,3584]{1,0:T(8,128)(2,1)} %pack_rows.1.beside, f32[128,1]{1,0:T(8,128)} %fusion.4.keep, f32[1,3584]{1,0:T(1,128)} %gain.1, ...), custom_call_target="tpu_custom_call" | custom-call | flops 1024 | bytes 1024 | tf_op jit(solution)/shard_map/expert_update/pallas_call | solution.py:274
  38.1 7.1 %merge_rows.3 = bf16[256,3584]{1,0:T(8,128)(2,1)} custom-call(s32[1,1024]{1,0:T(1,128)} %and_select_fusion.pos.slots, bf16[1024,3584]{1,0:T(8,128)(2,1)} %bitcast.22, bf16[128,3584]{1,0:T(8,128)(2,1)} %get-tuple-element.17.changed), custom_call_target="tpu_custom_call" | custom-call | flops 1024 | bytes 1024 | tf_op jit(solution)/shard_map/merge_rows/pallas_call | solution.py:121
  45.2 1.5 collective-permute-start
  46.8 7.1 %merge_rows.4 = bf16[256,3584]{1,0:T(8,128)(2,1)} custom-call(s32[1,1024]{1,0:T(1,128)} %and_select_fusion.pos.slots, bf16[1024,3584]{1,0:T(8,128)(2,1)} %bitcast.23, bf16[128,3584]{1,0:T(8,128)(2,1)} %get-tuple-element.17.changed), custom_call_target="tpu_custom_call" | custom-call | flops 1024 | bytes 1024 | tf_op jit(solution)/shard_map/merge_rows/pallas_call | solution.py:121
  53.9 2.7 %collective-permute-done.2.early = bf16[272,3584]{1,0:T(8,128)(2,1)S(1)} collective-permute-done((bf16[272,3584]{1,0:T(8,128)(2,1)}, bf16[272,3584]{1,0:T(8,128)(2,1)S(1)}, u32[]{:S(2)}, u32[]{:S(2)}) %collective-permute-start.2) | collective-permute-done | bytes 1949728 | tf_op jit(solution)/shard_map/ppermute | solution.py:19
  56.6 0.0 copy-start
  56.6 0.0 collective-permute-start.3
  56.6 0.5 collective-permute-start.4
  57.1 4.4 %merge_rows.5 = bf16[128,3584]{1,0:T(8,128)(2,1)} custom-call(s32[1,1024]{1,0:T(1,128)} %and_select_fusion.pos.slots, bf16[1024,3584]{1,0:T(8,128)(2,1)} %bitcast.24, bf16[128,3584]{1,0:T(8,128)(2,1)} %get-tuple-element.17.changed), custom_call_target="tpu_custom_call" | custom-call | flops 1024 | bytes 1024 | tf_op jit(solution)/shard_map/merge_rows/pallas_call | solution.py:121
  61.4 34.5 %collective-permute-done.piece = bf16[256,3584]{1,0:T(8,128)(2,1)S(1)} collective-permute-done((bf16[256,3584]{1,0:T(8,128)(2,1)}, bf16[256,3584]{1,0:T(8,128)(2,1)S(1)}, u32[]{:S(2)}, u32[]{:S(2)}) %collective-permute-start) | collective-permute-done | bytes 1835040 | tf_op jit(solution)/shard_map/ppermute | solution.py:19
  95.9 0.0 collective-permute-start.1
  95.9 0.0 copy-done
  96.0 0.6 copy.17
  96.6 58.4 %collective-permute-done.4.late = bf16[128,3584]{1,0:T(8,128)(2,1)S(1)} collective-permute-done((bf16[128,3584]{1,0:T(8,128)(2,1)}, bf16[128,3584]{1,0:T(8,128)(2,1)S(1)}, u32[]{:S(2)}, u32[]{:S(2)}) %collective-permute-start.4) | collective-permute-done | bytes 917536 | tf_op jit(solution)/shard_map/ppermute | solution.py:19
  154.9 0.0 copy-start.1
  154.9 0.9 copy-done.1
  155.8 5.2 %unpack_rows.1._ = bf16[1024,3584]{1,0:T(8,128)(2,1)} custom-call(s32[1,384]{1,0:T(1,128)} %bitcast.30, bf16[272,3584]{1,0:T(8,128)(2,1)} %copy-done, bf16[128,3584]{1,0:T(8,128)(2,1)} %copy-done.1), custom_call_target="tpu_custom_call" | custom-call | flops 1024 | bytes 1024 | tf_op jit(solution)/shard_map/unpack_rows/pallas_call | solution.py:151
  161.0 1.2 put_rows.3._
  162.3 0.0 collective-permute-done.3.piece
  162.3 1.2 put_rows.4._
  163.5 10.2 %collective-permute-done.1.piece = bf16[128,3584]{1,0:T(8,128)(2,1)S(1)} collective-permute-done((bf16[128,3584]{1,0:T(8,128)(2,1)}, bf16[128,3584]{1,0:T(8,128)(2,1)S(1)}, u32[]{:S(2)}, u32[]{:S(2)}) %collective-permute-start.1) | collective-permute-done | bytes 917536 | tf_op jit(solution)/shard_map/ppermute | solution.py:19
  173.8 0.9 put_rows.5
  (5 shorter events, 0.0 us)
Async XLA Ops:
  6.2 50.4 %collective-permute-start.2 = (bf16[272,3584]{1,0:T(8,128)(2,1)}, bf16[272,3584]{1,0:T(8,128)(2,1)S(1)}, u32[]{:S(2)}, u32[]{:S(2)}) collective-permute-start(bf16[272,3584]{1,0:T(8,128)(2,1)} %pack_early.1), channel_id=1, source_target_pairs={{0,2},{2,4},{4,6},{6,8},{8,10},{10,12},{12,14},{14,16},{16,18},{18... | collective-permute-start | bytes 5849096 | tf_op jit(solution)/shard_map/ppermute | solution.py:19
  16.5 6.6 %copy-start.2 = (s32[1,1024]{1,0:T(1,128)S(1)}, s32[1,1024]{1,0:T(1,128)}, u32[]{:S(2)}) copy-start(s32[1,1024]{1,0:T(1,128)} %and_select_fusion.pos.slots) | copy-start | bytes 12292
  16.5 6.6 %copy-start.3 = (s32[1,1,1024,8]{2,3,1,0:T(8,128)S(1)}, s32[1,1,1024,8]{2,3,1,0:T(8,128)}, u32[]{:S(2)}) copy-start(s32[1,1,1024,8]{2,3,1,0:T(8,128)} %param.13) | copy-start | bytes 98308
  45.2 50.7 %collective-permute-start = (bf16[256,3584]{1,0:T(8,128)(2,1)}, bf16[256,3584]{1,0:T(8,128)(2,1)S(1)}, u32[]{:S(2)}, u32[]{:S(2)}) collective-permute-start(bf16[256,3584]{1,0:T(8,128)(2,1)} %merge_rows.3), channel_id=1, source_target_pairs={{0,2},{2,4},{4,6},{6,8},{8,10},{10,12},{12,14},{14,16},{16,18},{18... | collective-permute-start | bytes 5505032 | tf_op jit(solution)/shard_map/ppermute | solution.py:19
  56.6 39.3 %copy-start = (bf16[272,3584]{1,0:T(8,128)(2,1)}, bf16[272,3584]{1,0:T(8,128)(2,1)S(1)}, u32[]{:S(2)}) copy-start(bf16[272,3584]{1,0:T(8,128)(2,1)S(1)} %collective-permute-done.2.early) | copy-start | bytes 5849092
  56.6 105.6 %collective-permute-start.3 = (bf16[256,3584]{1,0:T(8,128)(2,1)}, bf16[256,3584]{1,0:T(8,128)(2,1)S(1)}, u32[]{:S(2)}, u32[]{:S(2)}) collective-permute-start(bf16[256,3584]{1,0:T(8,128)(2,1)} %merge_rows.4), channel_id=1, source_target_pairs={{0,2},{2,4},{4,6},{6,8},{8,10},{10,12},{12,14},{14,16},{16,18},{18... | collective-permute-start | bytes 5505032 | tf_op jit(solution)/shard_map/ppermute | solution.py:19
  56.6 98.3 %collective-permute-start.4 = (bf16[128,3584]{1,0:T(8,128)(2,1)}, bf16[128,3584]{1,0:T(8,128)(2,1)S(1)}, u32[]{:S(2)}, u32[]{:S(2)}) collective-permute-start(bf16[128,3584]{1,0:T(8,128)(2,1)} %get-tuple-element.20), channel_id=1, source_target_pairs={{0,2},{2,4},{4,6},{6,8},{8,10},{10,12},{12,14},{14,16},{16,18},{18... | collective-permute-start | bytes 2752520 | tf_op jit(solution)/shard_map/ppermute | solution.py:19
  95.9 77.8 %collective-permute-start.1 = (bf16[128,3584]{1,0:T(8,128)(2,1)}, bf16[128,3584]{1,0:T(8,128)(2,1)S(1)}, u32[]{:S(2)}, u32[]{:S(2)}) collective-permute-start(bf16[128,3584]{1,0:T(8,128)(2,1)} %merge_rows.5), channel_id=1, source_target_pairs={{0,2},{2,4},{4,6},{6,8},{8,10},{10,12},{12,14},{14,16},{16,18},{18... | collective-permute-start | bytes 2752520 | tf_op jit(solution)/shard_map/ppermute | solution.py:19
  154.9 0.9 copy-start.1
